TPU v7x, 32 devices: a whole 2x2x4 slice. The times are simulated.
32 devices in a mesh: dp: 8 (over z, x), mp: 4 (over y, core).
Axes of the slice: x: 2, y: 2, z: 4, core: 2. Of those that a mesh axis runs over, the one named last changes fastest.
Arguments:
- hidden_in: bfloat16 [1024, 16384], P('mp', 'dp'), may hold values from -6 to 6
- segment_ids: int32 [16384], P('dp'), may hold values from 0 to 15, never falling along the last dimension, each value on 1 to 2000 neighbouring positions
- w_query: bfloat16 [1024, 1024], P(None, 'mp'), may hold values from -0.1875 to 0.1875
- b_query: bfloat16 [1024], P('mp'), may hold values from -3 to 3
- w_key: bfloat16 [1024, 1024], P(None, 'mp'), may hold values from -0.1875 to 0.1875
- w_value: bfloat16 [1024, 1024], P(None, 'mp'), may hold values from -0.1875 to 0.1875
- b_value: bfloat16 [1024], P('mp'), may hold values from -3 to 3
- w_out: bfloat16 [1024, 1024], P('mp'), may hold values from -3 to 3
- b_out: bfloat16 [1024], P('mp'), may hold values from -3 to 3
- gain_one: bfloat16 [1024], P('mp'), may hold values from 0.25 to 1.75
- shift_one: bfloat16 [1024], P('mp'), may hold values from -3 to 3
- w_up: bfloat16 [1024, 4096], P(None, 'mp'), may hold values from -0.1875 to 0.1875
- b_up: bfloat16 [4096], P('mp'), may hold values from -3 to 3
- w_down: bfloat16 [4096, 1024], P('mp'), may hold values from -0.09375 to 0.09375
- b_down: bfloat16 [1024], P('mp'), may hold values from -3 to 3
- gain_two: bfloat16 [1024], P('mp'), may hold values from 0.25 to 1.75
- shift_two: bfloat16 [1024], P('mp'), may hold values from -3 to 3
- cotangent: bfloat16 [1024, 16384], P('mp', 'dp'), may hold values from -6 to 6
Outputs:
- layer_out: bfloat16 [1024, 16384], P('mp', 'dp')
- input_grad: bfloat16 [1024, 16384], P('mp', 'dp')
- grad_w_query: float32 [1024, 1024], P(None, 'mp')
- grad_b_query: float32 [1024], P('mp')
- grad_w_key: float32 [1024, 1024], P(None, 'mp')
- grad_w_value: float32 [1024, 1024], P(None, 'mp')
- grad_b_value: float32 [1024], P('mp')
- grad_w_out: float32 [1024, 1024], P('mp')
- grad_b_out: float32 [1024], P('mp')
- grad_gain_one: float32 [1024], P('mp')
- grad_shift_one: float32 [1024], P('mp')
- grad_w_up: float32 [1024, 4096], P(None, 'mp')
- grad_b_up: float32 [4096], P('mp')
- grad_w_down: float32 [4096, 1024], P('mp')
- grad_b_down: float32 [1024], P('mp')
- grad_gain_two: float32 [1024], P('mp')
- grad_shift_two: float32 [1024], P('mp')
Inputs may be any that keep to these rules, and one draw needn't show every extreme that they name: `segment_ids`: document numbers never fall along the tokens; each of the 16 numbers occurs on 1 to 2000 consecutive tokens, and some document has exactly 2000. A document may cross the border of two sequences; attention never does.
All inputs are finite; a program needn't handle non-finite values.
Results may differ from a plain program's by a relative error of at most 0.02.
Values may be sent and summed in bfloat16 or wider, within the bound.
No kernel may reach another device: no remote copies, remote signals or barrier semaphores. Data moves between devices by JAX's collectives and lax.ppermute only.
A program may use at most 384 MiB of HBM per device.

v0:
```python
import math

import jax
import jax.numpy as jnp
from jax import lax
from jax.sharding import PartitionSpec as P

D = 1024
HEADS = 16
HEAD = 64
SEQ_LEN = 2048


EPS = 1e-05
NEG = -1e30


def lead_dot(left, right):
    return lax.dot_general(
        left, right, (((0,), (0,)), ((), ())), preferred_element_type=jnp.float32
    )


def tail_dot(left, right):
    return lax.dot_general(
        left, right, (((1,), (1,)), ((), ())), preferred_element_type=jnp.float32
    )


def norm_rows(values, norm_gain, norm_shift):
    centre = values - jnp.mean(values, axis=0, keepdims=True)
    inverse = lax.rsqrt(jnp.mean(centre * centre, axis=0, keepdims=True) + EPS)
    normed = centre * inverse
    return (normed * norm_gain[:, None] + norm_shift[:, None], normed, inverse)


def norm_back(grad_rows, normed, inverse, norm_gain):
    scaled = grad_rows * norm_gain[:, None]
    return inverse * (
        scaled
        - jnp.mean(scaled, axis=0, keepdims=True)
        - normed * jnp.mean(scaled * normed, axis=0, keepdims=True)
    )


def masked_scores(left, right, seg_left, seg_right, factor):
    scores = jnp.einsum("dsq,dsk->sqk", left, right, preferred_element_type=jnp.float32) * factor
    return jnp.where(seg_left[:, :, None] == seg_right[:, None, :], scores, NEG)


def body(
    hidden_in,
    segment_ids,
    w_query,
    b_query,
    w_key,
    w_value,
    b_value,
    w_out,
    b_out,
    gain_one,
    shift_one,
    w_up,
    b_up,
    w_down,
    b_down,
    gain_two,
    shift_two,
    cotangent,
):
    part_count = lax.axis_size("mp")
    own_index = lax.axis_index("mp")
    width_here, group_len = hidden_in.shape
    seq_count = group_len // SEQ_LEN
    slice_len = SEQ_LEN // part_count
    own_count = seq_count * slice_len
    factor = 1.0 / math.sqrt(HEAD)

    def to_slices(rows):
        return rows.reshape(width_here, seq_count, part_count, slice_len)

    inputs_low, cot_low = (
        lax.all_to_all(to_slices(hidden_in), "mp", split_axis=2, concat_axis=0, tiled=True),
        lax.all_to_all(to_slices(cotangent), "mp", split_axis=2, concat_axis=0, tiled=True),
    )
    full_query, full_key, full_value, full_up = (
        lax.all_gather(w_query, "mp", axis=1, tiled=True),
        lax.all_gather(w_key, "mp", axis=1, tiled=True),
        lax.all_gather(w_value, "mp", axis=1, tiled=True),
        lax.all_gather(w_up, "mp", axis=1, tiled=True),
    )
    (
        full_out,
        full_down,
        bias_query,
        bias_value,
        bias_out,
        gain_first,
        shift_first,
        bias_up,
        bias_down,
        gain_second,
        shift_second,
    ) = [
        piece.astype(jnp.float32) if piece.ndim == 1 else piece
        for piece in (
            lax.all_gather(w_out, "mp", axis=0, tiled=True),
            lax.all_gather(w_down, "mp", axis=0, tiled=True),
            lax.all_gather(b_query, "mp", axis=0, tiled=True),
            lax.all_gather(b_value, "mp", axis=0, tiled=True),
            lax.all_gather(b_out, "mp", axis=0, tiled=True),
            lax.all_gather(gain_one, "mp", axis=0, tiled=True),
            lax.all_gather(shift_one, "mp", axis=0, tiled=True),
            lax.all_gather(b_up, "mp", axis=0, tiled=True),
            lax.all_gather(b_down, "mp", axis=0, tiled=True),
            lax.all_gather(gain_two, "mp", axis=0, tiled=True),
            lax.all_gather(shift_two, "mp", axis=0, tiled=True),
        )
    ]
    inputs = inputs_low.reshape(D, own_count)
    seg_full = segment_ids.reshape(seq_count, SEQ_LEN)
    seg_own = lax.dynamic_slice_in_dim(
        seg_full.reshape(seq_count, part_count, slice_len), own_index, 1, 1
    )
    seg_own = seg_own.reshape(seq_count, slice_len)
    query_low = (lead_dot(full_query, inputs) + bias_query[:, None]).astype(jnp.bfloat16)
    key_low = lead_dot(full_key, inputs).astype(jnp.bfloat16)
    value_low = (lead_dot(full_value, inputs) + bias_value[:, None]).astype(jnp.bfloat16)
    key_full, value_full = (
        lax.all_gather(key_low.reshape(D, seq_count, 1, slice_len), "mp", axis=2, tiled=True),
        lax.all_gather(value_low.reshape(D, seq_count, 1, slice_len), "mp", axis=2, tiled=True),
    )

    def own_heads(rows):
        return rows.reshape(HEADS, HEAD, seq_count, slice_len)

    def full_heads(rows):
        return rows.reshape(HEADS, HEAD, seq_count, SEQ_LEN)

    query_heads = own_heads(query_low)
    key_heads = full_heads(key_full)
    value_heads = full_heads(value_full)

    def attend(pieces):
        head_query, head_key, head_value = pieces
        scores = masked_scores(head_query, head_key, seg_own, seg_full, factor)
        highest = jnp.max(scores, axis=-1, keepdims=True)
        raised = jnp.exp(scores - highest)
        row_total = jnp.sum(raised, axis=-1, keepdims=True)
        softened = (raised / row_total).astype(jnp.bfloat16)
        context_head = jnp.einsum(
            "sqk,dsk->dsq", softened, head_value, preferred_element_type=jnp.float32
        )
        return (context_head, (highest + jnp.log(row_total))[..., 0])

    context_heads, log_totals = lax.map(attend, (query_heads, key_heads, value_heads))
    context = context_heads.reshape(D, own_count).astype(jnp.bfloat16)
    first_sum = inputs.astype(jnp.float32) + (lead_dot(full_out, context) + bias_out[:, None])
    first_out, normed_first, inverse_one = norm_rows(first_sum, gain_first, shift_first)
    first_low = first_out.astype(jnp.bfloat16)
    upward = lead_dot(full_up, first_low) + bias_up[:, None]
    activated = jax.nn.gelu(upward, approximate=False).astype(jnp.bfloat16)
    second_sum = first_out + (lead_dot(full_down, activated) + bias_down[:, None])
    final_rows, normed_second, inverse_two = norm_rows(second_sum, gain_second, shift_second)
    layer_low = final_rows.astype(jnp.bfloat16)
    grad_rows = cot_low.reshape(D, own_count).astype(jnp.float32)
    grad_shift_two = jnp.sum(grad_rows, axis=1)
    grad_gain_two = jnp.sum(grad_rows * normed_second, axis=1)
    second_grad = norm_back(grad_rows, normed_second, inverse_two, gain_second)
    grad_b_down = jnp.sum(second_grad, axis=1)
    down_low = second_grad.astype(jnp.bfloat16)
    grad_w_down = tail_dot(activated, down_low)
    act_grad = jnp.dot(full_down, down_low, preferred_element_type=jnp.float32)
    gelu_back = jax.vjp(lambda inner: jax.nn.gelu(inner, approximate=False), upward)[1]
    up_low = gelu_back(act_grad)[0].astype(jnp.bfloat16)
    grad_b_up = jnp.sum(up_low.astype(jnp.float32), axis=1)
    grad_w_up = tail_dot(first_low, up_low)
    first_grad = second_grad + jnp.dot(full_up, up_low, preferred_element_type=jnp.float32)
    grad_shift_one = jnp.sum(first_grad, axis=1)
    grad_gain_one = jnp.sum(first_grad * normed_first, axis=1)
    attn_grad = norm_back(first_grad, normed_first, inverse_one, gain_first)
    grad_b_out = jnp.sum(attn_grad, axis=1)
    out_low = attn_grad.astype(jnp.bfloat16)
    grad_w_out = tail_dot(context, out_low)
    context_grad = jnp.dot(full_out, out_low, preferred_element_type=jnp.float32).astype(
        jnp.bfloat16
    )
    grad_heads = own_heads(context_grad)

    def head_terms(head_query, head_key, head_value, head_grad, head_log):
        scores = masked_scores(head_query, head_key, seg_own, seg_full, factor)
        softened = jnp.exp(scores - head_log[..., None])
        prob_grad = jnp.einsum(
            "dsq,dsk->sqk", head_grad, head_value, preferred_element_type=jnp.float32
        )
        centre = jnp.sum(softened * prob_grad, axis=-1, keepdims=True)
        score_grad = (softened * (prob_grad - centre)).astype(jnp.bfloat16)
        query_part = (
            jnp.einsum("sqk,dsk->dsq", score_grad, head_key, preferred_element_type=jnp.float32)
            * factor
        )
        return (softened, score_grad, centre[..., 0], query_part)

    def back_head(pieces):
        head_query, head_key, head_value, head_grad, head_log = pieces
        softened, score_grad, centre, query_part = head_terms(
            head_query, head_key, head_value, head_grad, head_log
        )
        key_part = (
            jnp.einsum("sqk,dsq->dsk", score_grad, head_query, preferred_element_type=jnp.float32)
            * factor
        )
        value_part = jnp.einsum(
            "sqk,dsq->dsk",
            softened.astype(jnp.bfloat16),
            head_grad,
            preferred_element_type=jnp.float32,
        )
        return (query_part, key_part, value_part)

    query_grad, key_part, value_part = lax.map(
        back_head, (query_heads, key_heads, value_heads, grad_heads, log_totals)
    )
    stacked = jnp.stack([key_part, value_part]).reshape(2, D, seq_count, part_count, slice_len)
    key_sums = lax.psum_scatter(
        stacked.astype(jnp.bfloat16), "mp", scatter_dimension=3, tiled=True
    ).astype(jnp.float32)
    key_grad = key_sums[0].reshape(D, own_count)
    value_grad = key_sums[1].reshape(D, own_count)
    dquery_low = query_grad.reshape(D, own_count).astype(jnp.bfloat16)
    dkey_low = key_grad.astype(jnp.bfloat16)
    dvalue_low = value_grad.astype(jnp.bfloat16)
    grad_b_query = jnp.sum(dquery_low.astype(jnp.float32), axis=1)
    grad_b_value = jnp.sum(dvalue_low.astype(jnp.float32), axis=1)
    grad_w_query = tail_dot(inputs, dquery_low)
    grad_w_key = tail_dot(inputs, dkey_low)
    grad_w_value = tail_dot(inputs, dvalue_low)
    input_low = (
        attn_grad
        + jnp.dot(full_query, dquery_low, preferred_element_type=jnp.float32)
        + jnp.dot(full_key, dkey_low, preferred_element_type=jnp.float32)
        + jnp.dot(full_value, dvalue_low, preferred_element_type=jnp.float32)
    ).astype(jnp.bfloat16)
    out_pair = (
        lax.all_to_all(
            layer_low.reshape(D, seq_count, 1, slice_len),
            "mp",
            split_axis=0,
            concat_axis=2,
            tiled=True,
        ),
        lax.all_to_all(
            input_low.reshape(D, seq_count, 1, slice_len),
            "mp",
            split_axis=0,
            concat_axis=2,
            tiled=True,
        ),
    )
    layer_out = out_pair[0].reshape(width_here, group_len)
    input_grad = out_pair[1].reshape(width_here, group_len)
    col_grads = (
        lax.psum_scatter(
            grad_w_query.astype(jnp.bfloat16), "mp", scatter_dimension=1, tiled=True
        ).astype(jnp.float32),
        lax.psum_scatter(
            grad_w_key.astype(jnp.bfloat16), "mp", scatter_dimension=1, tiled=True
        ).astype(jnp.float32),
        lax.psum_scatter(
            grad_w_value.astype(jnp.bfloat16), "mp", scatter_dimension=1, tiled=True
        ).astype(jnp.float32),
        lax.psum_scatter(
            grad_w_up.astype(jnp.bfloat16), "mp", scatter_dimension=1, tiled=True
        ).astype(jnp.float32),
    )
    row_grads = (
        lax.psum_scatter(
            grad_w_out.astype(jnp.bfloat16), "mp", scatter_dimension=0, tiled=True
        ).astype(jnp.float32),
        lax.psum_scatter(
            grad_w_down.astype(jnp.bfloat16), "mp", scatter_dimension=0, tiled=True
        ).astype(jnp.float32),
        lax.psum_scatter(
            grad_b_query.astype(jnp.bfloat16), "mp", scatter_dimension=0, tiled=True
        ).astype(jnp.float32),
        lax.psum_scatter(
            grad_b_value.astype(jnp.bfloat16), "mp", scatter_dimension=0, tiled=True
        ).astype(jnp.float32),
        lax.psum_scatter(
            grad_b_out.astype(jnp.bfloat16), "mp", scatter_dimension=0, tiled=True
        ).astype(jnp.float32),
        lax.psum_scatter(
            grad_gain_one.astype(jnp.bfloat16), "mp", scatter_dimension=0, tiled=True
        ).astype(jnp.float32),
        lax.psum_scatter(
            grad_shift_one.astype(jnp.bfloat16), "mp", scatter_dimension=0, tiled=True
        ).astype(jnp.float32),
        lax.psum_scatter(
            grad_b_up.astype(jnp.bfloat16), "mp", scatter_dimension=0, tiled=True
        ).astype(jnp.float32),
        lax.psum_scatter(
            grad_b_down.astype(jnp.bfloat16), "mp", scatter_dimension=0, tiled=True
        ).astype(jnp.float32),
        lax.psum_scatter(
            grad_gain_two.astype(jnp.bfloat16), "mp", scatter_dimension=0, tiled=True
        ).astype(jnp.float32),
        lax.psum_scatter(
            grad_shift_two.astype(jnp.bfloat16), "mp", scatter_dimension=0, tiled=True
        ).astype(jnp.float32),
    )
    summed = (
        lax.psum(col_grads[0].astype(jnp.bfloat16), "dp").astype(jnp.float32),
        lax.psum(row_grads[2].astype(jnp.bfloat16), "dp").astype(jnp.float32),
        lax.psum(col_grads[1].astype(jnp.bfloat16), "dp").astype(jnp.float32),
        lax.psum(col_grads[2].astype(jnp.bfloat16), "dp").astype(jnp.float32),
        lax.psum(row_grads[3].astype(jnp.bfloat16), "dp").astype(jnp.float32),
        lax.psum(row_grads[0].astype(jnp.bfloat16), "dp").astype(jnp.float32),
        lax.psum(row_grads[4].astype(jnp.bfloat16), "dp").astype(jnp.float32),
        lax.psum(row_grads[5].astype(jnp.bfloat16), "dp").astype(jnp.float32),
        lax.psum(row_grads[6].astype(jnp.bfloat16), "dp").astype(jnp.float32),
        lax.psum(col_grads[3].astype(jnp.bfloat16), "dp").astype(jnp.float32),
        lax.psum(row_grads[7].astype(jnp.bfloat16), "dp").astype(jnp.float32),
        lax.psum(row_grads[1].astype(jnp.bfloat16), "dp").astype(jnp.float32),
        lax.psum(row_grads[8].astype(jnp.bfloat16), "dp").astype(jnp.float32),
        lax.psum(row_grads[9].astype(jnp.bfloat16), "dp").astype(jnp.float32),
        lax.psum(row_grads[10].astype(jnp.bfloat16), "dp").astype(jnp.float32),
    )
    return (layer_out, input_grad) + tuple(summed)


def solution(mesh):
    in_specs = (
        P("mp", "dp"),
        P("dp"),
        P(None, "mp"),
        P("mp"),
        P(None, "mp"),
        P(None, "mp"),
        P("mp"),
        P("mp", None),
        P("mp"),
        P("mp"),
        P("mp"),
        P(None, "mp"),
        P("mp"),
        P("mp", None),
        P("mp"),
        P("mp"),
        P("mp"),
        P("mp", "dp"),
    )
    out_specs = (
        P("mp", "dp"),
        P("mp", "dp"),
        P(None, "mp"),
        P("mp"),
        P(None, "mp"),
        P(None, "mp"),
        P("mp"),
        P("mp", None),
        P("mp"),
        P("mp"),
        P("mp"),
        P(None, "mp"),
        P("mp"),
        P("mp", None),
        P("mp"),
        P("mp"),
        P("mp"),
    )
    return jax.shard_map(body, mesh=mesh, in_specs=in_specs, out_specs=out_specs, check_vma=False)
```

profile of v0, /device:TPU:0, one launch (start us, length us, event | category | flops | bytes accessed | tf_op | source)
XLA Modules:
  0.0 1160.2 jit_solution(17227462185844552605)
XLA Ops:
  15.9 24.2 %all-gather.2 = bf16[4,1,256]{2,1,0:T(2,128)(2,1)S(1)} all-gather(bf16[1,1,256]{2,1,0:T(2,128)(2,1)S(1)} %reshape.336), channel_id=1, replica_groups=mesh['dp'=8,'mp'=4] {'mp'}, dimensions={0}, use_global_device_ids=true | all-gather | bytes 2560 | tf_op jit(solution)/shard_map/all_gather | solution.py:110
  47.4 21.5 %all-gather.23.cloned.1.call-done = bf16[1024,1024]{1,0:T(8,128)(2,1)} async-done(((bf16[1024,256]{1,0:T(8,128)(2,1)}), bf16[1024,1024]{1,0:T(8,128)(2,1)}) %all-gather.23.cloned.1.call-update) | async-done | bytes 2097168 | tf_op jit(solution)/shard_map/all_gather | solution.py:88
  79.9 23.8 %all-gather.8 = bf16[4,1,256]{2,1,0:T(2,128)(2,1)S(1)} all-gather(bf16[1,1,256]{2,1,0:T(2,128)(2,1)S(1)} %reshape.348), channel_id=1, replica_groups=mesh['dp'=8,'mp'=4] {'mp'}, dimensions={0}, use_global_device_ids=true | all-gather | bytes 2560 | tf_op jit(solution)/shard_map/all_gather | solution.py:116
  113.9 5.1 all-gather.5
  118.9 5.1 all-gather.6
  124.0 5.2 all_gather.63
  129.2 5.1 all-gather.7
  146.0 30.1 %all-gather.33.cloned.1.call-done = bf16[1024,2048]{1,0:T(8,128)(2,1)} async-done(((bf16[1024,512]{1,0:T(8,128)(2,1)}), bf16[1024,2048]{1,0:T(8,128)(2,1)}) %all-gather.33.cloned.1.call-update) | async-done | bytes 4194320 | tf_op jit(solution)/shard_map/all_gather | solution.py:130
  176.2 73.8 %while.26 = (s32[]{:T(128)}, bf16[16,64,1,512]{3,1,2,0:T(8,128)(2,1)S(1)}, f32[16,1,512]{2,1,0:T(1,128)S(1)}, bf16[16,64,1,2048]{3,1,2,0:T(8,128)(2,1)}, s32[1,1...) while((s32[]{:T(128)}, ...), condition=%wide.region_3.4_spmd, body=%wide.region_0.3_spmd.sunk | while | flops 277872128 | bytes 13336673 | solution.py:156
  255.0 5.1 all-gather.27.cloned.1.call-done
  260.0 27.5 %fusion.47 = (bf16[4096,512]{0,1:T(8,128)(2,1)}, f32[4096,512]{0,1:T(8,128)}, f32[512,4096]{1,0:T(8,128)}) fusion(f32[4096]{0:T(1024)S(1)} %convert_element_type.263, bf16[1024,4096]{1,0:T(8,128)(2,1)} %all-gather.27.cloned.1.call-done, f32[1024,512]{0,1:T(8,128)S(1)} %get-tuple-element.420, f32[1024]{0:T(1024)S(1)} %bitcast.365, f32[1024]{0:T(1024)S(1)} %bitcast.356, ...), kind=kOutput, calls=%fused_computation.68 | convolution fusion | flops 4436000768 | bytes 31485952 | tf_op jit(solution)/shard_map/dot_general | solution.py:19
  287.5 32.4 %all-gather.29.cloned.1.call-done = bf16[4096,1024]{1,0:T(8,128)(2,1)} async-done(((bf16[1024,1024]{1,0:T(8,128)(2,1)}), bf16[4096,1024]{1,0:T(8,128)(2,1)}) %all-gather.29.cloned.1.call-update) | async-done | bytes 8388624 | tf_op jit(solution)/shard_map/all_gather | solution.py:108
  319.9 9.0 fusion.84
  331.8 14.2 %fusion.85 = (bf16[4096]{0:T(1024)(128)(2,1)S(1)}, bf16[4096,512]{0,1:T(8,128)(2,1)S(1)}) fusion(f32[4096,512]{0,1:T(8,128)} %get-tuple-element.413, bf16[4096,1024]{1,0:T(8,128)(2,1)} %all-gather.29.cloned.1.call-done, f32[1024,512]{0,1:T(8,128)S(1)} %get-tuple-element.409, f32[512,4096]{1,0:T(8,128)} %get-tuple-element.421, ...), kind=kOutput, calls=%fused_computation.147 | convolution fusion | flops 4329041920 | bytes 31481856 | tf_op jit(solution)/shard_map/dot_general | solution.py:173
  346.0 9.2 multiply_reduce_fusion.2
  360.0 168.9 %while.27 = (s32[]{:T(128)}, bf16[16,64,1,512]{3,1,2,0:T(8,128)(2,1)S(1)}, bf16[16,64,1,2048]{3,1,2,0:T(8,128)(2,1)}, bf16[16,64,1,2048]{3,1,2,0:T(8,128)(2,1)},...) while((s32[]{:T(128)}, ...), condition=%wide.region_14.15_spmd, body=%wide.region_12.14_spmd.sunk | while | flops 681737728 | bytes 33711224 | solution.py:221
  528.9 8.2 stack.10
  537.1 7.9 stack.9
  545.0 8.7 pad_maximum_fusion
  553.7 8.3 copy.133
  570.9 10.2 convolution_convert_fusion.1
  582.7 9.3 convolution_convert_fusion
  592.0 41.9 %reduce-scatter.8.cloned.1.call-done = bf16[2,1024,1,1,512]{4,1,2,0,3:T(8,128)(2,1)} async-done(((bf16[2,1024,1,4,512]{4,1,2,0,3:T(8,128)(2,1)}), bf16[2,1024,1,1,512]{4,1,2,0,3:T(8,128)(2,1)}) %reduce-scatter.8.cloned.1.call-update) | async-done | bytes 2097168 | tf_op jit(solution)/shard_map/reduce_scatter | solution.py:225
  640.6 27.3 %reduce-scatter.16.cloned.1.call-done = bf16[256,1024]{1,0:T(8,128)(2,1)} async-done(((bf16[1024,1024]{1,0:T(8,128)(2,1)}), bf16[256,1024]{1,0:T(8,128)(2,1)}) %reduce-scatter.16.cloned.1.call-update) | async-done | bytes 524304 | tf_op jit(solution)/shard_map/reduce_scatter | solution.py:277
  667.9 34.6 %reduce-scatter.10.cloned.1.call-done = bf16[1024,256]{0,1:T(8,128)(2,1)} async-done(((bf16[1024,1024]{0,1:T(8,128)(2,1)}), bf16[1024,256]{0,1:T(8,128)(2,1)}) %reduce-scatter.10.cloned.1.call-update) | async-done | bytes 524304 | tf_op jit(solution)/shard_map/reduce_scatter | solution.py:263
  702.5 74.4 %reduce-scatter.18.cloned.1.call-done = bf16[1024,1024]{1,0:T(8,128)(2,1)} async-done(((bf16[1024,4096]{1,0:T(8,128)(2,1)}), bf16[1024,1024]{1,0:T(8,128)(2,1)}) %reduce-scatter.18.cloned.1.call-update) | async-done | bytes 2097168 | tf_op jit(solution)/shard_map/reduce_scatter | solution.py:272
  776.9 74.3 %reduce-scatter.20.cloned.1.call-done = bf16[1024,1024]{1,0:T(8,128)(2,1)} async-done(((bf16[4096,1024]{1,0:T(8,128)(2,1)}), bf16[1024,1024]{1,0:T(8,128)(2,1)}) %reduce-scatter.20.cloned.1.call-update) | async-done | bytes 2097168 | tf_op jit(solution)/shard_map/reduce_scatter | solution.py:280
  851.2 34.6 %reduce-scatter.12.cloned.1.call-done = bf16[1024,256]{0,1:T(8,128)(2,1)} async-done(((bf16[1024,1024]{0,1:T(8,128)(2,1)}), bf16[1024,256]{0,1:T(8,128)(2,1)}) %reduce-scatter.12.cloned.1.call-update) | async-done | bytes 524304 | tf_op jit(solution)/shard_map/reduce_scatter | solution.py:266
  885.8 33.8 %reduce-scatter.14.cloned.1.call-done = bf16[1024,256]{0,1:T(8,128)(2,1)} async-done(((bf16[1024,1024]{0,1:T(8,128)(2,1)}), bf16[1024,256]{0,1:T(8,128)(2,1)}) %reduce-scatter.14.cloned.1.call-update) | async-done | bytes 524304 | tf_op jit(solution)/shard_map/reduce_scatter | solution.py:269
  958.2 12.7 %all-reduce.11 = (bf16[1024]{0:T(1024)(128)(2,1)S(1)}, bf16[1024]{0:T(1024)(128)(2,1)S(1)}, bf16[1024]{0:T(1024)(128)(2,1)S(1)}, bf16[1024]{0:T(1024)(128)(2,1)S...) all-reduce(bf16[1024]{0:T(1024)(128)(2,1)S(1)} %reduce_sum.196, ...), channel_id=6, replica_groups=mesh['dp'=8,'mp'=4] {'mp'}, use_global_device_ids=true, to_apply=%region_19.20.clone | all-reduce | flops 12288 | bytes 49152
  971.6 23.4 %all-reduce.9 = (bf16[256]{0:T(256)(128)(2,1)S(1)}, bf16[256]{0:T(256)(128)(2,1)S(1)}, bf16[256]{0:T(256)(128)(2,1)S(1)}, bf16[256]{0:T(256)(128)(2,1)S(1)}, bf1...) all-reduce(bf16[256]{0:T(256)(128)(2,1)S(1)} %dynamic-slice.1, ...), channel_id=1, replica_groups=mesh['dp'=8,'mp'=4] {'dp'}, use_global_device_ids=true, to_apply=%region_20.21 | all-reduce | flops 3072 | bytes 12288 | tf_op jit(solution)/shard_map/psum | solution.py:313
  1003.3 138.5 %all-reduce.14.cloned.1.call-done = (bf16[1024,256]{0,1:T(8,128)(2,1)}, bf16[1024,256]{0,1:T(8,128)(2,1)}, bf16[1024,256]{0,1:T(8,128)(2,1)}, bf16[256,1024]{1,0...) async-done(((bf16[1024,256]{0,1:T(8,128)(2,1)}, bf16[1024,256]{0,1:T(8,128)(2,1)}, bf16[1024,256]{0,1:T(8,128)(2,1)}, bf16[256,1024]{1,0:T(8,128)(2,1)}, ...) | async-done | bytes 6291472 | tf_op jit(solution)/shard_map/psum | solution.py:312
  (420 shorter events, 377.1 us)
Async XLA Ops:
  7.2 36.2 %all-gather.19.cloned.1.call-start = ((), (), s32[]{:S(2)}) async-start(), calls=%async_computation.11 | async-start | bytes 2621440 | tf_op jit(solution)/shard_map/all_gather | solution.py:89
  7.9 60.9 %all-gather.23.cloned.1.call-start = ((), (), s32[]{:S(2)}) async-start(), calls=%async_computation.13 | async-start | bytes 2621440 | tf_op jit(solution)/shard_map/all_gather | solution.py:88
  8.7 134.4 %all-gather.21.cloned.1.call-start = ((), (), s32[]{:S(2)}) async-start(), calls=%async_computation.12 | async-start | bytes 2621440 | tf_op jit(solution)/shard_map/all_gather | solution.py:87
  11.7 28.4 %all-to-all-start = ((bf16[256,1,4,512]{0,3,1,2:T(8,128)(2,1)}), bf16[256,1,4,512]{0,3,1,2:T(8,128)(2,1)S(1)}, u32[]{:S(2)}, u32[]{:S(2)}) async-start(bf16[256,1,4,512]{0,3,1,2:T(8,128)(2,1)} %bitcast.15), calls=%async_computation | async-start | bytes 2097152 | tf_op jit(solution)/shard_map/all_to_all | solution.py:83
  15.9 130.1 %all-gather.31.cloned.1.call-start = ((), (), s32[]{:S(2)}) async-start(), calls=%async_computation.24 | async-start | bytes 5242880 | tf_op jit(solution)/shard_map/all_gather | solution.py:131
  41.2 210.1 %copy-start.10 = (bf16[64,8,4,256]{3,1,2,0:T(8,128)(2,1)}, bf16[64,8,4,256]{3,1,2,0:T(8,128)(2,1)S(1)}, u32[]{:S(2)}) copy-start(bf16[64,8,4,256]{3,1,2,0:T(8,128)(2,1)S(1)} %copy.145) | copy-start | bytes 3145732
  47.3 128.8 %all-gather.33.cloned.1.call-start = ((), (), s32[]{:S(2)}) async-start(), calls=%async_computation.25 | async-start | bytes 5242880 | tf_op jit(solution)/shard_map/all_gather | solution.py:130
  72.7 177.3 %all-gather.25.cloned.1.call-start = ((), (), s32[]{:S(2)}) async-start(), calls=%async_computation.14 | async-start | bytes 2621440 | tf_op jit(solution)/shard_map/all_gather | solution.py:107
  73.3 30.3 %copy-start.26 = (s32[2048]{0:T(1024)S(1)}, s32[2048]{0:T(1024)}, u32[]{:S(2)}) copy-start(s32[2048]{0:T(1024)} %param.23) | copy-start | bytes 24580
  73.3 30.3 %copy-start.31 = (bf16[256]{0:T(256)(128)(2,1)S(1)}, bf16[256]{0:T(256)(128)(2,1)}, u32[]{:S(2)}) copy-start(bf16[256]{0:T(256)(128)(2,1)} %param.25) | copy-start | bytes 1540
  73.3 35.4 %copy-start.32 = (bf16[256]{0:T(256)(128)(2,1)S(1)}, bf16[256]{0:T(256)(128)(2,1)}, u32[]{:S(2)}) copy-start(bf16[256]{0:T(256)(128)(2,1)} %param.30) | copy-start | bytes 1540
  73.4 40.5 %copy-start.33 = (bf16[256]{0:T(256)(128)(2,1)S(1)}, bf16[256]{0:T(256)(128)(2,1)}, u32[]{:S(2)}) copy-start(bf16[256]{0:T(256)(128)(2,1)} %param.31) | copy-start | bytes 1540
  73.4 45.6 %copy-start.34 = (bf16[256]{0:T(256)(128)(2,1)S(1)}, bf16[256]{0:T(256)(128)(2,1)}, u32[]{:S(2)}) copy-start(bf16[256]{0:T(256)(128)(2,1)} %param.32) | copy-start | bytes 1540
  73.4 50.6 %copy-start.27 = (bf16[1024]{0:T(1024)(128)(2,1)S(1)}, bf16[1024]{0:T(1024)(128)(2,1)}, u32[]{:S(2)}) copy-start(bf16[1024]{0:T(1024)(128)(2,1)} %param.34) | copy-start | bytes 6148
  73.4 55.8 %copy-start.35 = (bf16[256]{0:T(256)(128)(2,1)S(1)}, bf16[256]{0:T(256)(128)(2,1)}, u32[]{:S(2)}) copy-start(bf16[256]{0:T(256)(128)(2,1)} %param.36) | copy-start | bytes 1540
  73.4 60.9 %copy-start.36 = (bf16[256]{0:T(256)(128)(2,1)S(1)}, bf16[256]{0:T(256)(128)(2,1)}, u32[]{:S(2)}) copy-start(bf16[256]{0:T(256)(128)(2,1)} %param.38) | copy-start | bytes 1540
  73.4 186.6 %all-gather.27.cloned.1.call-start = ((), (), s32[]{:S(2)}) async-start(), calls=%async_computation.15 | async-start | bytes 10485760 | tf_op jit(solution)/shard_map/all_gather | solution.py:90
  75.5 63.9 %all-to-all-start.2 = ((bf16[256,1,4,512]{0,3,1,2:T(8,128)(2,1)}), bf16[256,1,4,512]{0,3,1,2:T(8,128)(2,1)S(1)}, u32[]{:S(2)}, u32[]{:S(2)}) async-start(bf16[256,1,4,512]{0,3,1,2:T(8,128)(2,1)} %bitcast.40), calls=%async_computation.2 | async-start | bytes 2097152 | tf_op jit(solution)/shard_map/all_to_all | solution.py:84
  79.0 240.9 %all-gather.29.cloned.1.call-start = ((), (), s32[]{:S(2)}) async-start(), calls=%async_computation.16 | async-start | bytes 10485760 | tf_op jit(solution)/shard_map/all_gather | solution.py:108
  79.8 554.2 %reduce-scatter.8.cloned.1.call-start = ((), (), s32[]{:S(2)}) async-start(), calls=%async_computation.17 | async-start | bytes 10485760 | tf_op jit(solution)/shard_map/reduce_scatter | solution.py:225
  528.9 37.7 %copy-start.6 = (bf16[16,64,1,512]{3,1,2,0:T(8,128)(2,1)}, bf16[16,64,1,512]{3,1,2,0:T(8,128)(2,1)S(1)}, u32[]{:S(2)}) copy-start(bf16[16,64,1,512]{3,1,2,0:T(8,128)(2,1)S(1)} %get-tuple-element.121) | copy-start | bytes 3145732
  562.1 105.9 %reduce-scatter.16.cloned.1.call-start = ((), (), s32[]{:S(2)}) async-start(), calls=%async_computation.21 | async-start | bytes 2621440 | tf_op jit(solution)/shard_map/reduce_scatter | solution.py:277
  566.6 135.9 %reduce-scatter.10.cloned.1.call-start = ((), (), s32[]{:S(2)}) async-start(), calls=%async_computation.18 | async-start | bytes 2621440 | tf_op jit(solution)/shard_map/reduce_scatter | solution.py:263
  570.8 206.0 %reduce-scatter.18.cloned.1.call-start = ((), (), s32[]{:S(2)}) async-start(), calls=%async_computation.22 | async-start | bytes 10485760 | tf_op jit(solution)/shard_map/reduce_scatter | solution.py:272
  581.1 270.1 %reduce-scatter.20.cloned.1.call-start = ((), (), s32[]{:S(2)}) async-start(), calls=%async_computation.23 | async-start | bytes 10485760 | tf_op jit(solution)/shard_map/reduce_scatter | solution.py:280
  591.9 42.0 %copy-start.11 = (bf16[64,8,4,256]{3,1,2,0:T(8,128)(2,1)S(1)}, bf16[64,8,4,256]{3,1,2,0:T(8,128)(2,1)}, u32[]{:S(2)}) copy-start(bf16[64,8,4,256]{3,1,2,0:T(8,128)(2,1)} %copy-done.10) | copy-start | bytes 3145732
  592.0 293.8 %reduce-scatter.12.cloned.1.call-start = ((), (), s32[]{:S(2)}) async-start(), calls=%async_computation.19 | async-start | bytes 2621440 | tf_op jit(solution)/shard_map/reduce_scatter | solution.py:266
  637.9 281.7 %reduce-scatter.14.cloned.1.call-start = ((), (), s32[]{:S(2)}) async-start(), calls=%async_computation.20 | async-start | bytes 2621440 | tf_op jit(solution)/shard_map/reduce_scatter | solution.py:269
  640.6 279.6 %copy-start.9 = (bf16[1024,1,1,512]{0,3,2,1:T(8,128)(2,1)S(1)}, bf16[1024,1,1,512]{0,3,2,1:T(8,128)(2,1)}, u32[]{:S(2)}) copy-start(bf16[1024,1,1,512]{0,3,2,1:T(8,128)(2,1)} %get-tuple-element.418) | copy-start | bytes 3145732
  640.6 501.3 %all-reduce.14.cloned.1.call-start = ((), (), s32[]{:S(2)}) async-start(), calls=%async_computation.26 | async-start | bytes 12582912 | tf_op jit(solution)/shard_map/psum | solution.py:312
  924.3 18.6 %all-to-all-start.1 = ((bf16[4,2,65536]{2,1,0:T(2,128)(2,1)}), bf16[4,2,65536]{2,1,0:T(2,128)(2,1)S(1)}, u32[]{:S(2)}, u32[]{:S(2)}) async-start(bf16[4,2,65536]{2,1,0:T(2,128)(2,1)} %reshape.370), calls=%async_computation.1 | async-start | bytes 2097152 | tf_op jit(solution)/shard_map/all_to_all | solution.py:245
  943.8 56.3 %all-to-all-start.3 = ((bf16[4,2,65536]{2,1,0:T(2,128)(2,1)}), bf16[4,2,65536]{2,1,0:T(2,128)(2,1)S(1)}, u32[]{:S(2)}, u32[]{:S(2)}) async-start(bf16[4,2,65536]{2,1,0:T(2,128)(2,1)} %reshape.372), calls=%async_computation.4 | async-start | bytes 2097152 | tf_op jit(solution)/shard_map/all_to_all | solution.py:252
  (27 other events, 170.3 us)
Sparse Core Ops, SparseCore 0:
  9.6 33.7 all-gather.18
  45.0 23.8 all-gather.22
  70.4 32.2 all-gather.20
  104.6 34.9 all-gather.30
  141.6 34.4 all-gather.32
  177.5 22.5 all-gather.24
  201.7 58.2 all-gather.26
  261.6 58.2 all-gather.28
  562.2 71.7 reduce-scatter.7
  636.5 31.4 reduce-scatter.15
  671.0 31.4 reduce-scatter.9
  705.1 71.7 reduce-scatter.17
  779.5 71.7 reduce-scatter.19
  854.3 31.4 reduce-scatter.11
  888.2 31.4 reduce-scatter.13
  925.3 216.5 all-reduce.13
where the time goes:
time: 1170 us; the launch traced here: 1160 us
  waiting for transfers between devices  555 us (47%)
  matrix products  338 us (29%)
  blocking collectives  120 us (10%)
  local copies, waits for them, and re-layouts  64.3 us (5%)
  other arithmetic  50 us (4%)
  between operations  16.4 us (1%)
  starting transfers between devices  15.7 us (1%)
    psum x1, waiting for transfers between devices, body(): lax.psum(col_grads[0].astype(jnp.bfloat16), 'dp').astype(jnp.float32)  139 us
    reduce_scatter x1, waiting for transfers between devices, body(): lax.psum_scatter(grad_w_up.astype(jnp.bfloat16), 'mp', scatter_dimension=...  74.4 us
    reduce_scatter x1, waiting for transfers between devices, body(): lax.psum_scatter(grad_w_down.astype(jnp.bfloat16), 'mp', scatter_dimensio...  74.3 us
    dot_general x32, matrix products, masked_scores(): jnp.einsum('dsq,dsk->sqk', left, right, preferred_element_type=jnp.float32)  70.6 us
    dot_general x6, matrix products, lead_dot(): lax.dot_general(left, right, (((0,), (0,)), ((), ())), preferred_element_...  50.4 us
    reduce_scatter x1, waiting for transfers between devices, body(): lax.psum_scatter(stacked.astype(jnp.bfloat16), 'mp', scatter_dimension=3,...  41.9 us
    dot_general x6, matrix products, tail_dot(): lax.dot_general(left, right, (((1,), (1,)), ((), ())), preferred_element_...  34.6 us
    reduce_scatter x1, waiting for transfers between devices, body(): lax.psum_scatter(grad_w_key.astype(jnp.bfloat16), 'mp', scatter_dimension...  34.6 us
  transfers between devices with their start and end apart: 20, of which 13 were waited for; matrix products, arithmetic and copies ran while one was open for 17% of the time, Pallas kernels for 0%

commit v1 on v0

v1 whole, which is shorter than its diff:
```python
import math

import jax
import jax.numpy as jnp
from jax import lax
from jax.experimental import pallas as pl
from jax.experimental.pallas import tpu as pltpu
from jax.sharding import PartitionSpec as P

D = 1024
HEADS = 16
HEAD = 64
SEQ_LEN = 2048

EPS = 1e-05
BIG = 1e30
Q_BLOCK = 256
K_CHUNK = 512
VMEM_LIMIT = 56 * 1024 * 1024

F32 = jnp.float32
BF16 = jnp.bfloat16


def lead_dot(left, right):
    return lax.dot_general(left, right, (((0,), (0,)), ((), ())), preferred_element_type=F32)


def tail_dot(left, right):
    return lax.dot_general(left, right, (((1,), (1,)), ((), ())), preferred_element_type=F32)


def dot(left, right):
    return jnp.dot(left, right, preferred_element_type=F32)


def swap(piece, axis, mask):
    count = lax.axis_size(axis)
    return lax.ppermute(piece, axis, [(i, i ^ mask) for i in range(count)])


def bits_of(axis):
    count, found, bit = lax.axis_size(axis), [], 1
    while bit < count:
        found.append(bit)
        bit *= 2
    return found


def gather_slots(piece, axis):
    slots = {0: piece}
    for bit in reversed(bits_of(axis)):
        for slot in sorted(slots):
            slots[slot | bit] = swap(slots[slot], axis, bit)
    return slots


def scatter_slots(slots, axis, wire=BF16):
    slots = dict(slots)
    for bit in bits_of(axis):
        for slot in sorted(slots, reverse=True):
            if slot & bit:
                moved = swap(slots.pop(slot).astype(wire), axis, bit)
                slots[slot ^ bit] = slots[slot ^ bit].astype(F32) + moved.astype(F32)
    return slots[0]


def place(slots, own, dim):
    count, width = len(slots), slots[0].shape[dim]
    shape = list(slots[0].shape)
    shape[dim] = width * count
    whole = jnp.zeros(shape, slots[0].dtype)
    for slot in sorted(slots):
        whole = lax.dynamic_update_slice_in_dim(whole, slots[slot], (own ^ slot) * width, dim)
    return whole


def cut(whole, own, slot, count, dim):
    width = whole.shape[dim] // count
    return lax.dynamic_slice_in_dim(whole, (own ^ slot) * width, width, dim)


def exchange(whole, own, axis, dim):
    count = lax.axis_size(axis)
    return {
        slot: swap(cut(whole, own, slot, count, dim), axis, slot)
        if slot
        else cut(whole, own, 0, count, dim)
        for slot in range(count)
    }


def sum_over(piece, axis, order):
    index = lax.axis_index(axis)
    trail = []
    for bit in order:
        upper = (index & bit) != 0
        half = piece.shape[0] // 2
        mine = lax.dynamic_slice_in_dim(piece, jnp.where(upper, half, 0), half, 0)
        other = lax.dynamic_slice_in_dim(piece, jnp.where(upper, 0, half), half, 0)
        got = swap(other, axis, bit)
        piece = (mine.astype(F32) + got.astype(F32)).astype(piece.dtype)
        trail.append((bit, upper))
    for bit, upper in reversed(trail):
        got = swap(piece, axis, bit)
        half = piece.shape[0]
        whole = jnp.concatenate([piece, piece], axis=0)
        piece = lax.dynamic_update_slice_in_dim(whole, got, jnp.where(upper, 0, half), 0)
    return piece


def sum_small(piece, axis):
    for bit in bits_of(axis):
        piece = piece + swap(piece, axis, bit)
    return piece


def sum_weights(piece, axis):
    order = bits_of(axis)
    rows = piece.shape[0] // 2
    return jnp.concatenate(
        [
            sum_over(piece[:rows], axis, order),
            sum_over(piece[rows:], axis, order[1:] + order[:1]),
        ],
        axis=0,
    )


def seg_codes(segment_ids):
    digits = jnp.arange(16, dtype=jnp.int32)[:, None]
    low = (segment_ids[None, :] & 15) == digits
    high = ((segment_ids[None, :] >> 4) & 15) == digits
    same = jnp.concatenate([low, high], axis=0)
    keys = same.astype(BF16)
    queries = jnp.where(same, 0.0, -BIG).astype(BF16)
    return keys, queries


def key_ranges(segment_ids, seq_count):
    rows = segment_ids.reshape(seq_count, 1, SEQ_LEN)
    blocks = segment_ids.reshape(seq_count, SEQ_LEN // Q_BLOCK, Q_BLOCK)
    first = jnp.sum((rows < blocks[:, :, :1]).astype(jnp.int32), axis=-1)
    last = jnp.sum((rows <= blocks[:, :, -1:]).astype(jnp.int32), axis=-1)
    return (first // K_CHUNK).reshape(-1), ((last + K_CHUNK - 1) // K_CHUNK).reshape(-1)


def attend_kernel(heads, from_ref, to_ref, q_ref, k_ref, v_ref, qc_ref, kc_ref, o_ref, lse_ref, kt, va, top, acc):
    seq, block = pl.program_id(0), pl.program_id(1)
    spot = seq * pl.num_programs(1) + block

    @pl.when(block == 0)
    def _():
        codes = kc_ref[...].astype(F32)
        for h in range(heads):
            rows = slice(h * HEAD, (h + 1) * HEAD)
            whole = jnp.concatenate([k_ref[rows, :].astype(F32), codes, jnp.zeros_like(codes)], axis=0)
            kt[h] = whole.T.astype(BF16)
            lines = lax.broadcasted_iota(jnp.int32, (16, SEQ_LEN), 0)
            va[h] = jnp.concatenate(
                [v_ref[rows, :], jnp.where(lines == 0, 1.0, 0.0).astype(BF16)], axis=0
            )

    top[...] = jnp.full_like(top, -BIG)
    acc[...] = jnp.zeros_like(acc)
    queries = []
    for h in range(heads):
        scaled = (q_ref[h * HEAD : (h + 1) * HEAD, :].astype(F32) * (1.0 / math.sqrt(HEAD))).astype(BF16)
        queries.append(
            jnp.concatenate([scaled, qc_ref[...], jnp.zeros((32, Q_BLOCK), BF16)], axis=0)
        )

    def step(chunk, carry):
        at = pl.multiple_of(chunk * K_CHUNK, K_CHUNK)
        for h in range(heads):
            scores = dot(kt[h, pl.ds(at, K_CHUNK), :], queries[h])
            before = top[h]
            highest = jnp.maximum(before, jnp.max(scores, axis=0, keepdims=True))
            raised = jnp.exp(scores - highest).astype(BF16)
            acc[h] = acc[h] * jnp.exp(before - highest) + dot(va[h, :, pl.ds(at, K_CHUNK)], raised)
            top[h] = highest
        return carry

    lax.fori_loop(from_ref[spot], to_ref[spot], step, 0)
    for h in range(heads):
        total = acc[h, HEAD : HEAD + 1, :]
        o_ref[h * HEAD : (h + 1) * HEAD, :] = (acc[h, :HEAD, :] / total).astype(BF16)
        lse_ref[0, h : h + 1, :] = top[h] + jnp.log(total)


def attend(queries, keys, values, codes_q, codes_k, ranges, seq_count):
    width, length = queries.shape
    heads = width // HEAD
    blocks = SEQ_LEN // Q_BLOCK
    by_block = lambda s, b, *_: (0, s * blocks + b)
    by_seq = lambda s, b, *_: (0, s)
    spec = pltpu.PrefetchScalarGridSpec(
        num_scalar_prefetch=2,
        grid=(seq_count, blocks),
        in_specs=[
            pl.BlockSpec((width, Q_BLOCK), by_block),
            pl.BlockSpec((width, SEQ_LEN), by_seq),
            pl.BlockSpec((width, SEQ_LEN), by_seq),
            pl.BlockSpec((32, Q_BLOCK), by_block),
            pl.BlockSpec((32, SEQ_LEN), by_seq),
        ],
        out_specs=[
            pl.BlockSpec((width, Q_BLOCK), by_block),
            pl.BlockSpec((1, heads, Q_BLOCK), lambda s, b, *_: (0, 0, s * blocks + b)),
        ],
        scratch_shapes=[
            pltpu.VMEM((heads, SEQ_LEN, 128), BF16),
            pltpu.VMEM((heads, HEAD + 16, SEQ_LEN), BF16),
            pltpu.VMEM((heads, 1, Q_BLOCK), F32),
            pltpu.VMEM((heads, HEAD + 16, Q_BLOCK), F32),
        ],
    )
    area = length * SEQ_LEN * heads
    return pl.pallas_call(
        lambda *refs: attend_kernel(heads, *refs),
        grid_spec=spec,
        out_shape=[
            jax.ShapeDtypeStruct((width, length), BF16),
            jax.ShapeDtypeStruct((1, heads, length), F32),
        ],
        compiler_params=pltpu.CompilerParams(
            dimension_semantics=("arbitrary", "arbitrary"), vmem_limit_bytes=VMEM_LIMIT
        ),
        cost_estimate=pl.CostEstimate(flops=12 * HEAD * area, bytes_accessed=8 * width * length, transcendentals=area),
        name="attend",
    )(*ranges, queries, keys, values, codes_q, codes_k)


def attend_back_kernel(
    heads, from_ref, to_ref, q_ref, o_ref, do_ref, lse_ref, k_ref, v_ref, qc_ref, kc_ref, dq_ref, dkv_ref, kt, vt, acc, dq_acc
):
    seq, block = pl.program_id(0), pl.program_id(1)
    spot = seq * pl.num_programs(1) + block

    @pl.when(block == 0)
    def _():
        codes = kc_ref[...].astype(F32)
        lines = lax.broadcasted_iota(jnp.int32, (16, SEQ_LEN), 0)
        ones = jnp.where(lines < 3, 1.0, 0.0).astype(F32)
        blank = jnp.zeros((16, SEQ_LEN), F32)
        for h in range(heads):
            rows = slice(h * HEAD, (h + 1) * HEAD)
            kt[h] = jnp.concatenate([k_ref[rows, :].astype(F32), codes, ones, blank], axis=0).T.astype(BF16)
            vt[h] = jnp.concatenate([v_ref[rows, :].astype(F32), ones, blank, blank, blank], axis=0).T.astype(BF16)
        acc[...] = jnp.zeros_like(acc)

    dq_acc[...] = jnp.zeros_like(dq_acc)
    lines = lax.broadcasted_iota(jnp.int32, (16, Q_BLOCK), 0)
    lanes = lax.broadcasted_iota(jnp.int32, (Q_BLOCK, 128), 1)
    blank = jnp.zeros((16, Q_BLOCK), BF16)

    def parts(row):
        first = row.astype(BF16)
        rest = row - first.astype(F32)
        second = rest.astype(BF16)
        third = (rest - second.astype(F32)).astype(BF16)
        spread = jnp.where(
            lines == 0,
            first.astype(F32),
            jnp.where(lines == 1, second.astype(F32), jnp.where(lines == 2, third.astype(F32), 0.0)),
        )
        return spread.astype(BF16)

    queries, grads, both = [], [], []
    for h in range(heads):
        rows = slice(h * HEAD, (h + 1) * HEAD)
        scaled = q_ref[rows, :].astype(F32) * (1.0 / math.sqrt(HEAD))
        grad = do_ref[rows, :].astype(F32)
        centre = jnp.sum(grad * o_ref[rows, :].astype(F32), axis=0, keepdims=True)
        queries.append(
            jnp.concatenate([scaled.astype(BF16), qc_ref[...], parts(-lse_ref[0, h : h + 1, :]), blank], axis=0)
        )
        grads.append(jnp.concatenate([do_ref[rows, :], parts(-centre), blank, blank, blank], axis=0))
        turned = jnp.concatenate([grad, scaled], axis=0).T
        both.append(
            jnp.concatenate(
                [jnp.where(lanes < HEAD, turned, 0.0), jnp.where(lanes < HEAD, 0.0, turned)], axis=0
            ).astype(BF16)
        )

    def step(chunk, carry):
        at = pl.multiple_of(chunk * K_CHUNK, K_CHUNK)
        span = pl.ds(at, K_CHUNK)
        for h in range(heads):
            softened = jnp.exp(dot(kt[h, span, :], queries[h]))
            shifted = dot(vt[h, span, :], grads[h])
            score_grad = (softened * shifted).astype(BF16)
            pair = jnp.concatenate([softened.astype(BF16), score_grad], axis=1)
            acc[h, span, :] += dot(pair, both[h])
            dq_acc[h] += dot(k_ref[h * HEAD : (h + 1) * HEAD, span], score_grad)
        return carry

    lax.fori_loop(from_ref[spot], to_ref[spot], step, 0)
    for h in range(heads):
        dq_ref[h * HEAD : (h + 1) * HEAD, :] = (dq_acc[h] * (1.0 / math.sqrt(HEAD))).astype(BF16)

    @pl.when(block == pl.num_programs(1) - 1)
    def _():
        for h in range(heads):
            dkv_ref[:, h * 128 : (h + 1) * 128] = acc[h].astype(BF16)


def attend_back(queries, context, grads, log_totals, keys, values, codes_q, codes_k, ranges, seq_count):
    width, length = queries.shape
    heads = width // HEAD
    blocks = SEQ_LEN // Q_BLOCK
    by_block = lambda s, b, *_: (0, s * blocks + b)
    by_seq = lambda s, b, *_: (0, s)
    spec = pltpu.PrefetchScalarGridSpec(
        num_scalar_prefetch=2,
        grid=(seq_count, blocks),
        in_specs=[
            pl.BlockSpec((width, Q_BLOCK), by_block),
            pl.BlockSpec((width, Q_BLOCK), by_block),
            pl.BlockSpec((width, Q_BLOCK), by_block),
            pl.BlockSpec((1, heads, Q_BLOCK), lambda s, b, *_: (0, 0, s * blocks + b)),
            pl.BlockSpec((width, SEQ_LEN), by_seq),
            pl.BlockSpec((width, SEQ_LEN), by_seq),
            pl.BlockSpec((32, Q_BLOCK), by_block),
            pl.BlockSpec((32, SEQ_LEN), by_seq),
        ],
        out_specs=[
            pl.BlockSpec((width, Q_BLOCK), by_block),
            pl.BlockSpec((SEQ_LEN, 2 * width), lambda s, b, *_: (s, 0)),
        ],
        scratch_shapes=[
            pltpu.VMEM((heads, SEQ_LEN, 128), BF16),
            pltpu.VMEM((heads, SEQ_LEN, 128), BF16),
            pltpu.VMEM((heads, SEQ_LEN, 128), F32),
            pltpu.VMEM((heads, HEAD, Q_BLOCK), F32),
        ],
    )
    area = length * SEQ_LEN * heads
    return pl.pallas_call(
        lambda *refs: attend_back_kernel(heads, *refs),
        grid_spec=spec,
        out_shape=[
            jax.ShapeDtypeStruct((width, length), BF16),
            jax.ShapeDtypeStruct((length, 2 * width), BF16),
        ],
        compiler_params=pltpu.CompilerParams(
            dimension_semantics=("arbitrary", "arbitrary"), vmem_limit_bytes=VMEM_LIMIT
        ),
        cost_estimate=pl.CostEstimate(flops=30 * HEAD * area, bytes_accessed=14 * width * length, transcendentals=area),
        name="attend_back",
    )(*ranges, queries, context, grads, log_totals, keys, values, codes_q, codes_k)


def norm_rows(values, norm_gain, norm_shift):
    centre = values - jnp.mean(values, axis=0, keepdims=True)
    inverse = lax.rsqrt(jnp.mean(centre * centre, axis=0, keepdims=True) + EPS)
    normed = centre * inverse
    return (normed * norm_gain[:, None] + norm_shift[:, None], normed, inverse)


def norm_back(grad_rows, normed, inverse, norm_gain):
    scaled = grad_rows * norm_gain[:, None]
    return inverse * (
        scaled
        - jnp.mean(scaled, axis=0, keepdims=True)
        - normed * jnp.mean(scaled * normed, axis=0, keepdims=True)
    )


def gelu_slope(upward):
    flat = (1.0 + lax.erf(upward * (1.0 / math.sqrt(2.0)))) * 0.5
    return flat + upward * jnp.exp(upward * upward * -0.5) * (1.0 / math.sqrt(2.0 * math.pi))


def body(
    hidden_in,
    segment_ids,
    w_query,
    b_query,
    w_key,
    w_value,
    b_value,
    w_out,
    b_out,
    gain_one,
    shift_one,
    w_up,
    b_up,
    w_down,
    b_down,
    gain_two,
    shift_two,
    cotangent,
):
    parts = lax.axis_size("mp")
    own = lax.axis_index("mp")
    width, length = hidden_in.shape
    seq_count = length // SEQ_LEN
    own_len = length // parts
    own_heads = width // HEAD

    inputs = place(gather_slots(hidden_in, "mp"), own, 0)
    vectors = jnp.stack([b_out, gain_one, shift_one, b_down, gain_two, shift_two])
    vectors = place(gather_slots(vectors, "mp"), own, 1).astype(F32)
    bias_out, gain_first, shift_first, bias_down, gain_second, shift_second = [vectors[i] for i in range(6)]
    out_slots = gather_slots(w_out, "mp")
    full_out = jnp.concatenate([out_slots[r] for r in range(parts)], axis=0)
    cot_own = place(exchange(cotangent, own, "mp", 1), own, 0)

    w_pair = jnp.concatenate(
        [w_value.reshape(D, own_heads, HEAD), w_key.reshape(D, own_heads, HEAD)], axis=2
    ).reshape(D, 2 * width)
    queries = (lead_dot(w_query, inputs) + b_query.astype(F32)[:, None]).astype(BF16)
    keys = lead_dot(w_key, inputs).astype(BF16)
    values = (lead_dot(w_value, inputs) + b_value.astype(F32)[:, None]).astype(BF16)
    codes_k, codes_q = seg_codes(segment_ids)
    ranges = key_ranges(segment_ids, seq_count)
    context, log_totals = attend(queries, keys, values, codes_q, codes_k, ranges, seq_count)

    context_slots = exchange(context, own, "mp", 1)
    context_own = jnp.concatenate([context_slots[r] for r in range(parts)], axis=0)
    inputs_own = lax.dynamic_slice_in_dim(inputs, own * own_len, own_len, 1)
    first_sum = inputs_own.astype(F32) + (lead_dot(full_out, context_own) + bias_out[:, None])
    first_out, normed_first, inverse_one = norm_rows(first_sum, gain_first, shift_first)

    first_low = gather_slots(first_out.astype(BF16), "mp")
    bias_up = b_up.astype(F32)[:, None]
    upward, activated, down_part = {}, {}, {}
    for r in range(parts):
        upward[r] = lead_dot(w_up, first_low[r]) + bias_up
        activated[r] = jax.nn.gelu(upward[r], approximate=False).astype(BF16)
        down_part[r] = lead_dot(w_down, activated[r])
        if r:
            down_part[r] = down_part[r].astype(BF16)
    second_sum = first_out + (scatter_slots(down_part, "mp") + bias_down[:, None])
    final_rows, normed_second, inverse_two = norm_rows(second_sum, gain_second, shift_second)
    layer_out = place(exchange(final_rows.astype(BF16), own, "mp", 0), own, 1)

    grad_rows = cot_own.astype(F32)
    grad_shift_two = jnp.sum(grad_rows, axis=1)
    grad_gain_two = jnp.sum(grad_rows * normed_second, axis=1)
    second_grad = norm_back(grad_rows, normed_second, inverse_two, gain_second)
    grad_b_down = jnp.sum(second_grad, axis=1)

    down_low = gather_slots(second_grad.astype(BF16), "mp")
    up_low, up_part = {}, {}
    for r in range(parts):
        up_low[r] = (dot(w_down, down_low[r]) * gelu_slope(upward[r])).astype(BF16)
        up_part[r] = dot(w_up, up_low[r])
        if r:
            up_part[r] = up_part[r].astype(BF16)
    joined = lambda slots: jnp.concatenate([slots[r] for r in range(parts)], axis=1)
    all_up = joined(up_low)
    grad_w_down = tail_dot(joined(activated), joined(down_low)).astype(BF16)
    grad_w_up = tail_dot(joined(first_low), all_up).astype(BF16)
    grad_b_up = jnp.sum(all_up.astype(F32), axis=1)
    sum_down = sum_weights(grad_w_down, "dp")
    sum_up = sum_weights(grad_w_up, "dp")

    first_grad = second_grad + scatter_slots(up_part, "mp")
    grad_shift_one = jnp.sum(first_grad, axis=1)
    grad_gain_one = jnp.sum(first_grad * normed_first, axis=1)
    attn_grad = norm_back(first_grad, normed_first, inverse_one, gain_first)
    grad_b_out = jnp.sum(attn_grad, axis=1)
    out_low = attn_grad.astype(BF16)
    context_grad = dot(full_out, out_low).astype(BF16)
    grad_heads = place(
        {r: swap(context_grad[r * width : (r + 1) * width], "mp", r) if r else context_grad[:width] for r in range(parts)},
        own,
        1,
    )
    out_part = tail_dot(context_own, out_low).astype(BF16)
    grad_w_out = scatter_slots({r: out_part[r * width : (r + 1) * width] for r in range(parts)}, "mp")
    sum_out = sum_weights(grad_w_out.astype(BF16), "dp")

    query_grad, pair_grad = attend_back(
        queries, context, grad_heads, log_totals, keys, values, codes_q, codes_k, ranges, seq_count
    )
    grad_b_query = jnp.sum(query_grad.astype(F32), axis=1)
    grad_pair = dot(inputs, pair_grad)
    grad_pair_bias = jnp.sum(pair_grad.astype(F32), axis=0)
    grad_w_query = tail_dot(inputs, query_grad)
    split_pair = grad_pair.reshape(D, own_heads, 2, HEAD)
    grad_w_value = split_pair[:, :, 0].reshape(D, width)
    grad_w_key = split_pair[:, :, 1].reshape(D, width)
    grad_b_value = grad_pair_bias.reshape(own_heads, 2, HEAD)[:, 0].reshape(width)

    input_part = {}
    for r in range(parts):
        rows_query = cut(w_query, own, r, parts, 0)
        rows_pair = cut(w_pair, own, r, parts, 0)
        part = dot(rows_query, query_grad) + tail_dot(rows_pair, pair_grad)
        low = part.astype(BF16)
        here = lax.dynamic_slice_in_dim(low, own * own_len, own_len, 1).astype(F32) + cut(attn_grad, own, r, parts, 0)
        input_part[r] = lax.dynamic_update_slice_in_dim(low, here.astype(BF16), own * own_len, 1)
    input_grad = scatter_slots(input_part, "mp").astype(BF16)

    sum_heads = sum_weights(jnp.concatenate([grad_w_query, grad_w_key, grad_w_value], axis=0).astype(BF16), "dp")

    mixed = jnp.stack([grad_b_out, grad_gain_one, grad_shift_one, grad_b_down, grad_gain_two, grad_shift_two])
    mixed = scatter_slots({r: cut(mixed, own, r, parts, 1) for r in range(parts)}, "mp", wire=F32)
    small = jnp.concatenate([mixed.reshape(-1), grad_b_query, grad_b_value, grad_b_up])
    small = sum_small(small, "dp")
    vec = [small[i * width : (i + 1) * width] for i in range(8)]
    return (
        layer_out,
        input_grad,
        sum_heads[:D].astype(F32),
        vec[6],
        sum_heads[D : 2 * D].astype(F32),
        sum_heads[2 * D :].astype(F32),
        vec[7],
        sum_out.astype(F32),
        vec[0],
        vec[1],
        vec[2],
        sum_up.astype(F32),
        small[8 * width :],
        sum_down.astype(F32),
        vec[3],
        vec[4],
        vec[5],
    )


def solution(mesh):
    in_specs = (
        P("mp", "dp"),
        P("dp"),
        P(None, "mp"),
        P("mp"),
        P(None, "mp"),
        P(None, "mp"),
        P("mp"),
        P("mp", None),
        P("mp"),
        P("mp"),
        P("mp"),
        P(None, "mp"),
        P("mp"),
        P("mp", None),
        P("mp"),
        P("mp"),
        P("mp"),
        P("mp", "dp"),
    )
    out_specs = (
        P("mp", "dp"),
        P("mp", "dp"),
        P(None, "mp"),
        P("mp"),
        P(None, "mp"),
        P(None, "mp"),
        P("mp"),
        P("mp", None),
        P("mp"),
        P("mp"),
        P("mp"),
        P(None, "mp"),
        P("mp"),
        P("mp", None),
        P("mp"),
        P("mp"),
        P("mp"),
    )
    return jax.shard_map(body, mesh=mesh, in_specs=in_specs, out_specs=out_specs, check_vma=False)
```

time: 1170 us -> 653 us (0.56)
  waiting for transfers between devices: 555 us -> 268 us
  matrix products: 338 us -> 104 us
  blocking collectives: 120 us -> 0 us
  Pallas kernels: 0 us -> 109 us
  starting transfers between devices: 15.7 us -> 69.3 us
  local copies, waits for them, and re-layouts: 64.3 us -> 49.7 us
  between operations: 16.4 us -> 2.87 us
  other arithmetic: 50 us -> 38 us
    reduce_scatter x7 -> x0, waiting for transfers between devices: 321 us -> none  [the longest x1 74.4 us: body(): lax.psum_scatter(grad_w_up.astype(jnp.bfloat16), 'mp', scatter_dimension=...]
    ppermute x0 -> x93, waiting for transfers between devices: none -> 268 us  [swap(): return lax.ppermute(piece, axis, [(i, i ^ mask) for i in range(count)])]
    dot_general x118 -> x14, matrix products: 253 us -> 31.3 us  [dot(): return jnp.dot(left, right, preferred_element_type=F32)]
    psum x1 -> x0, waiting for transfers between devices: 139 us -> none  [body(): lax.psum(col_grads[0].astype(jnp.bfloat16), 'dp').astype(jnp.float32)]
    pallas_call x0 -> x2, Pallas kernels: none -> 109 us  [the longest x1 57.7 us: attend(): pl.pallas_call(lambda *refs: attend_kernel(heads, *refs), grid_spec=spec,...]
    all_gather x8 -> x0, waiting for transfers between devices: 91.3 us -> none  [the longest x1 32.4 us: body(): lax.all_gather(w_down, 'mp', axis=0, tiled=True)]
    all_gather x9 -> x0, blocking collectives: 83.5 us -> none  [the longest x1 24.2 us: body(): lax.all_gather(b_value, 'mp', axis=0, tiled=True)]
    ppermute x0 -> x93, starting transfers between devices: none -> 69.3 us  [swap(): return lax.ppermute(piece, axis, [(i, i ^ mask) for i in range(count)])]
  transfers between devices with their start and end apart: 20 -> 93, of which waited for: 13 -> 47; matrix products, arithmetic and copies ran while one was open for 17% -> 22% of each run, Pallas kernels for 0% -> 17%
where the time goes in v1:
time: 653 us; the launch traced here: 641 us
  waiting for transfers between devices  268 us (41%)
  Pallas kernels  109 us (17%)
  matrix products  104 us (16%)
  starting transfers between devices  69.3 us (11%)
  local copies, waits for them, and re-layouts  49.7 us (8%)
  other arithmetic  38 us (6%)
    ppermute x93, waiting for transfers between devices, swap(): return lax.ppermute(piece, axis, [(i, i ^ mask) for i in range(count)])  268 us
    ppermute x93, starting transfers between devices, swap(): return lax.ppermute(piece, axis, [(i, i ^ mask) for i in range(count)])  69.3 us
    pallas_call x1, Pallas kernels, attend(): pl.pallas_call(lambda *refs: attend_kernel(heads, *refs), grid_spec=spec,...  57.7 us
    pallas_call x1, Pallas kernels, attend_back(): pl.pallas_call(lambda *refs: attend_back_kernel(heads, *refs), grid_spec=...  51.4 us
    dot_general x12, matrix products, lead_dot(): lax.dot_general(left, right, (((0,), (0,)), ((), ())), preferred_element_...  48.3 us
    dot_general x14, matrix products, dot(): return jnp.dot(left, right, preferred_element_type=F32)  31.3 us
    dot_general x8, matrix products, tail_dot(): lax.dot_general(left, right, (((1,), (1,)), ((), ())), preferred_element_...  24.2 us
  transfers between devices with their start and end apart: 93, of which 47 were waited for; matrix products, arithmetic and copies ran while one was open for 22% of the time, Pallas kernels for 17%

profile of v1, /device:TPU:0, one launch (start us, length us, event | category | flops | bytes accessed | tf_op | source)
XLA Modules:
  0.0 640.6 jit_solution(3531043457720398517)
XLA Ops:
  20.4 14.0 %collective-permute-done.1 = bf16[256,2048]{1,0:T(8,128)(2,1)} collective-permute-done((bf16[256,2048]{1,0:T(8,128)(2,1)}, bf16[256,2048]{1,0:T(8,128)(2,1)}, u32[]{:S(2)}, u32[]{:S(2)}) %collective-permute-start.1) | collective-permute-done | bytes 1048608 | tf_op jit(solution)/shard_map/ppermute | solution.py:39
  35.0 9.9 %collective-permute-done.4 = bf16[256,1024]{1,0:T(8,128)(2,1)S(1)} collective-permute-done((bf16[256,1024]{1,0:T(8,128)(2,1)}, bf16[256,1024]{1,0:T(8,128)(2,1)S(1)}, u32[]{:S(2)}, u32[]{:S(2)}) %collective-permute-start.4) | collective-permute-done | bytes 524320 | tf_op jit(solution)/shard_map/ppermute | solution.py:39
  50.7 4.5 fusion.32.refs_3_.refs_6_
  55.2 4.5 fusion.34.refs_2_
  64.2 57.7 %attend.1 = (bf16[256,2048]{1,0:T(8,128)(2,1)}, f32[1,4,2048]{2,1,0:T(4,128)}) custom-call(s32[8]{0:T(128)} %get-tuple-element.112.refs_0_, s32[8]{0:T(128)} %get-tuple-element.111.refs_1_, bf16[256,2048]{1,0:T(8,128)(2,1)} %fusion.34.refs_2_, bf16[256,2048]{1,0:T(8,128)(2,1)} %fusion.32.refs_3_.refs_6_, bf16[256,2048]{1,0:T(8,128)(2,1)} %fusion.33.refs_4_.refs_7_, ...), custom_call_target="tpu_custom_call" | custom-call | flops 12884901888 | bytes 4194304 | tf_op jit(solution)/shard_map/attend/pallas_call | solution.py:219
  126.8 4.6 collective-permute-done.8
  131.4 6.3 collective-permute-done.7
  141.7 24.1 %collective-permute-done.14 = bf16[1024,512]{1,0:T(8,128)(2,1)S(1)} collective-permute-done((bf16[1024,512]{1,0:T(8,128)(2,1)S(1)}, bf16[1024,512]{1,0:T(8,128)(2,1)S(1)}, u32[]{:S(2)}, u32[]{:S(2)}) %collective-permute-start.14) | collective-permute-done | bytes 1048608 | tf_op jit(solution)/shard_map/ppermute | solution.py:39
  170.9 23.0 %fusion.40 = (bf16[1024,512]{0,1:T(8,128)(2,1)S(1)}, bf16[1024,512]{0,1:T(8,128)(2,1)S(1)}, bf16[1024,512]{0,1:T(8,128)(2,1)S(1)}, bf16[1024,512]{0,1:T(8,128)(2,1)S(1)}, f32[512,1024]{1,0:T(8,128)}) fusion(f32[1024]{0:T(1024)S(1)} %convert_element_type.514, f32[512,1024]{1,0:T(8,128)S(1)} %fusion.202, f32[512,1024]{1,0:T(8,128)S(1)} %fusion.203, ...), kind=kOutput, calls=%fused_computation.57 | convolution fusion | flops 1212153856 | bytes 15732736 | tf_op jit(solution)/shard_map/dot_general | solution.py:26
  202.2 28.9 %collective-permute-done.22 = bf16[256,512]{1,0:T(8,128)(2,1)S(1)} collective-permute-done((bf16[256,512]{1,0:T(8,128)(2,1)S(1)}, bf16[256,512]{1,0:T(8,128)(2,1)S(1)}, u32[]{:S(2)}, u32[]{:S(2)}) %collective-permute-start.22) | collective-permute-done | bytes 262176 | tf_op jit(solution)/shard_map/ppermute | solution.py:39
  231.1 4.5 collective-permute-done.23
  252.9 13.8 %collective-permute-done.26 = bf16[1024,512]{1,0:T(8,128)(2,1)} collective-permute-done((bf16[1024,512]{1,0:T(8,128)(2,1)}, bf16[1024,512]{1,0:T(8,128)(2,1)}, u32[]{:S(2)}, u32[]{:S(2)}) %collective-permute-start.26) | collective-permute-done | bytes 1048608 | tf_op jit(solution)/shard_map/ppermute | solution.py:39
  282.7 4.5 fusion.139
  289.1 7.4 %fusion.134 = bf16[1024,1024]{1,0:T(8,128)(2,1)S(1)} fusion(bf16[1024,512]{1,0:T(8,128)(2,1)S(1)} %copy-done.53, bf16[1024,512]{1,0:T(8,128)(2,1)} %collective-permute-done.26, bf16[1024,512]{1,0:T(8,128)(2,1)} %collective-permute-done.24, bf16[1024,512]{1,0:T(8,128)(2,1)} %fusion.187, bf16[1024,512]{0,1:T(8,128)(2,1)} %copy-done.63, ...), kind=kOutput, calls=%fused_computation.218 | convolution fusion | flops 4329570304 | bytes 10485760 | tf_op jit(solution)/shard_map/dot_general | solution.py:30
  304.3 13.9 %collective-permute-done.87 = bf16[256,1024]{1,0:T(8,128)(2,1)S(1)} collective-permute-done((bf16[256,1024]{1,0:T(8,128)(2,1)S(1)}, bf16[256,1024]{1,0:T(8,128)(2,1)S(1)}, u32[]{:S(2)}, u32[]{:S(2)}) %collective-permute-start.87) | collective-permute-done | bytes 524320 | tf_op jit(solution)/shard_map/ppermute | solution.py:39
  321.0 10.7 %collective-permute-done.70 = bf16[128,1024]{1,0:T(8,128)(2,1)S(1)} collective-permute-done((bf16[128,1024]{1,0:T(8,128)(2,1)S(1)}, bf16[128,1024]{1,0:T(8,128)(2,1)S(1)}, u32[]{:S(2)}, u32[]{:S(2)}) %collective-permute-start.70) | collective-permute-done | bytes 262176 | tf_op jit(solution)/shard_map/ppermute | solution.py:39
  334.1 5.5 collective-permute-done.82
  345.1 5.3 collective-permute-done.83
  361.1 6.3 collective-permute-done.84
  367.6 7.3 %collective-permute-done.79 = bf16[128,1024]{1,0:T(8,128)(2,1)S(1)} collective-permute-done((bf16[128,1024]{1,0:T(8,128)(2,1)S(1)}, bf16[128,1024]{1,0:T(8,128)(2,1)S(1)}, u32[]{:S(2)}, u32[]{:S(2)}) %collective-permute-start.79) | collective-permute-done | bytes 262176 | tf_op jit(solution)/shard_map/ppermute | solution.py:39
  383.8 9.8 %collective-permute-done.80 = bf16[256,1024]{1,0:T(8,128)(2,1)S(1)} collective-permute-done((bf16[256,1024]{1,0:T(8,128)(2,1)S(1)}, bf16[256,1024]{1,0:T(8,128)(2,1)S(1)}, u32[]{:S(2)}, u32[]{:S(2)}) %collective-permute-start.80) | collective-permute-done | bytes 524320 | tf_op jit(solution)/shard_map/ppermute | solution.py:39
  394.3 7.6 %collective-permute-done.92 = bf16[256,1024]{1,0:T(8,128)(2,1)S(1)} collective-permute-done((bf16[256,1024]{1,0:T(8,128)(2,1)S(1)}, bf16[256,1024]{1,0:T(8,128)(2,1)S(1)}, u32[]{:S(2)}, u32[]{:S(2)}) %collective-permute-start.92) | collective-permute-done | bytes 524320 | tf_op jit(solution)/shard_map/ppermute | solution.py:39
  407.0 5.9 collective-permute-done.29
  432.4 5.2 collective-permute-done.31
  444.2 51.4 %attend_back.1 = (bf16[256,2048]{1,0:T(8,128)(2,1)}, bf16[2048,512]{1,0:T(8,128)(2,1)}) custom-call(s32[8]{0:T(128)} %get-tuple-element.112.refs_0_, s32[8]{0:T(128)} %get-tuple-element.111.refs_1_, bf16[256,2048]{1,0:T(8,128)(2,1)} %fusion.34.refs_2_, bf16[256,2048]{1,0:T(8,128)(2,1)} %get-tuple-element.21.refs_3_, bf16[256,2048]{1,0:T(8,128)(2,1)} %copy-done.31, ...), custom_call_target="tpu_custom_call" | custom-call | flops 32212254720 | bytes 7340032 | tf_op jit(solution)/shard_map/attend_back/pallas_call | solution.py:339
  500.5 4.6 convolution_convert_fusion.9
  550.5 9.7 %collective-permute-done.49 = bf16[384,256]{1,0:T(8,128)(2,1)S(1)} collective-permute-done((bf16[384,256]{1,0:T(8,128)(2,1)S(1)}, bf16[384,256]{1,0:T(8,128)(2,1)S(1)}, u32[]{:S(2)}, u32[]{:S(2)}) %collective-permute-start.49) | collective-permute-done | bytes 196640 | tf_op jit(solution)/shard_map/ppermute | solution.py:39
  560.3 5.9 collective-permute-done.37
  571.8 5.4 collective-permute-done.38
  582.0 8.6 %collective-permute-done.39 = bf16[192,256]{1,0:T(8,128)(2,1)S(1)} collective-permute-done((bf16[192,256]{1,0:T(8,128)(2,1)S(1)}, bf16[192,256]{1,0:T(8,128)(2,1)S(1)}, u32[]{:S(2)}, u32[]{:S(2)}) %collective-permute-start.39) | collective-permute-done | bytes 98336 | tf_op jit(solution)/shard_map/ppermute | solution.py:39
  598.0 4.9 collective-permute-done.57
  631.9 5.2 collective-permute-done.41
  (513 shorter events, 256.7 us)
Async XLA Ops:
  7.9 37.0 %collective-permute-start = (bf16[256,2048]{1,0:T(8,128)(2,1)}, bf16[256,2048]{1,0:T(8,128)(2,1)}, u32[]{:S(2)}, u32[]{:S(2)}) collective-permute-start(bf16[256,2048]{1,0:T(8,128)(2,1)} %param.18), channel_id=1, source_target_pairs={{0,1},{1,0},{2,3},{3,2},{4,5},{5,4},{6,7},{7,6},{8,9},{9,8},{10,11... | collective-permute-start | bytes 3145736 | tf_op jit(solution)/shard_map/ppermute | solution.py:39
  8.1 26.3 %collective-permute-start.1 = (bf16[256,2048]{1,0:T(8,128)(2,1)}, bf16[256,2048]{1,0:T(8,128)(2,1)}, u32[]{:S(2)}, u32[]{:S(2)}) collective-permute-start(bf16[256,2048]{1,0:T(8,128)(2,1)} %param.18), channel_id=1, source_target_pairs={{0,2},{1,3},{2,0},{3,1},{4,6},{5,7},{6,4},{7,5},{8,10},{9,11},{10,... | collective-permute-start | bytes 3145736 | tf_op jit(solution)/shard_map/ppermute | solution.py:39
  8.3 117.3 %collective-permute-start.3 = (bf16[256,1024]{1,0:T(8,128)(2,1)}, bf16[256,1024]{1,0:T(8,128)(2,1)}, u32[]{:S(2)}, u32[]{:S(2)}) collective-permute-start(bf16[256,1024]{1,0:T(8,128)(2,1)} %param.25), channel_id=1, source_target_pairs={{0,1},{1,0},{2,3},{3,2},{4,5},{5,4},{6,7},{7,6},{8,9},{9,8},{10,11... | collective-permute-start | bytes 1572872 | tf_op jit(solution)/shard_map/ppermute | solution.py:39
  18.4 26.5 %collective-permute-start.4 = (bf16[256,1024]{1,0:T(8,128)(2,1)}, bf16[256,1024]{1,0:T(8,128)(2,1)S(1)}, u32[]{:S(2)}, u32[]{:S(2)}) collective-permute-start(bf16[256,1024]{1,0:T(8,128)(2,1)} %param.25), channel_id=1, source_target_pairs={{0,2},{1,3},{2,0},{3,1},{4,6},{5,7},{6,4},{7,5},{8,10},{9,11},{10,... | collective-permute-start | bytes 1572872 | tf_op jit(solution)/shard_map/ppermute | solution.py:39
  44.9 81.8 %collective-permute-start.5 = (bf16[256,1024]{1,0:T(8,128)(2,1)S(1)}, bf16[256,1024]{1,0:T(8,128)(2,1)S(1)}, u32[]{:S(2)}, u32[]{:S(2)}) collective-permute-start(bf16[256,1024]{1,0:T(8,128)(2,1)S(1)} %collective-permute-done.4), channel_id=1, source_target_pairs={{0,1},{1,0},{2,3},{3,2},{4,5},{5,4},{6,7},{7,6},{8,9},{9,8},{10,11... | collective-permute-start | bytes 1572872 | tf_op jit(solution)/shard_map/ppermute | solution.py:39
  141.2 24.6 %collective-permute-start.14 = (bf16[1024,512]{1,0:T(8,128)(2,1)S(1)}, bf16[1024,512]{1,0:T(8,128)(2,1)S(1)}, u32[]{:S(2)}, u32[]{:S(2)}) collective-permute-start(bf16[1024,512]{1,0:T(8,128)(2,1)S(1)} %fusion.142), channel_id=1, source_target_pairs={{0,2},{1,3},{2,0},{3,1},{4,6},{5,7},{6,4},{7,5},{8,10},{9,11},{10,... | collective-permute-start | bytes 3145736 | tf_op jit(solution)/shard_map/ppermute | solution.py:39
  141.7 25.5 %collective-permute-start.12 = (bf16[1024,512]{1,0:T(8,128)(2,1)S(1)}, bf16[1024,512]{1,0:T(8,128)(2,1)S(1)}, u32[]{:S(2)}, u32[]{:S(2)}) collective-permute-start(bf16[1024,512]{1,0:T(8,128)(2,1)S(1)} %fusion.142), channel_id=1, source_target_pairs={{0,1},{1,0},{2,3},{3,2},{4,5},{5,4},{6,7},{7,6},{8,9},{9,8},{10,11... | collective-permute-start | bytes 3145736 | tf_op jit(solution)/shard_map/ppermute | solution.py:39
  197.1 39.8 %collective-permute-start.13 = (bf16[1024,512]{1,0:T(8,128)(2,1)S(1)}, bf16[1024,512]{1,0:T(8,128)(2,1)S(1)}, u32[]{:S(2)}, u32[]{:S(2)}) collective-permute-start(bf16[1024,512]{1,0:T(8,128)(2,1)S(1)} %fusion.143), channel_id=1, source_target_pairs={{0,1},{1,0},{2,3},{3,2},{4,5},{5,4},{6,7},{7,6},{8,9},{9,8},{10,11... | collective-permute-start | bytes 3145736 | tf_op jit(solution)/shard_map/ppermute | solution.py:39
  199.4 37.5 %collective-permute-start.17 = (bf16[1024,512]{1,0:T(8,128)(2,1)S(1)}, bf16[1024,512]{1,0:T(8,128)(2,1)S(1)}, u32[]{:S(2)}, u32[]{:S(2)}) collective-permute-start(bf16[1024,512]{1,0:T(8,128)(2,1)S(1)} %fusion.66), channel_id=1, source_target_pairs={{0,2},{1,3},{2,0},{3,1},{4,6},{5,7},{6,4},{7,5},{8,10},{9,11},{10,... | collective-permute-start | bytes 3145736 | tf_op jit(solution)/shard_map/ppermute | solution.py:39
  200.3 30.7 %collective-permute-start.22 = (bf16[256,512]{1,0:T(8,128)(2,1)S(1)}, bf16[256,512]{1,0:T(8,128)(2,1)S(1)}, u32[]{:S(2)}, u32[]{:S(2)}) collective-permute-start(bf16[256,512]{1,0:T(8,128)(2,1)S(1)} %get-tuple-element.68), channel_id=1, source_target_pairs={{0,2},{1,3},{2,0},{3,1},{4,6},{5,7},{6,4},{7,5},{8,10},{9,11},{10,... | collective-permute-start | bytes 786440 | tf_op jit(solution)/shard_map/ppermute | solution.py:39
  201.9 33.7 %collective-permute-start.23 = (bf16[256,512]{1,0:T(8,128)(2,1)S(1)}, bf16[256,512]{1,0:T(8,128)(2,1)S(1)}, u32[]{:S(2)}, u32[]{:S(2)}) collective-permute-start(bf16[256,512]{1,0:T(8,128)(2,1)S(1)} %get-tuple-element.65), channel_id=1, source_target_pairs={{0,3},{1,2},{2,1},{3,0},{4,7},{5,6},{6,5},{7,4},{8,11},{9,10},{10,... | collective-permute-start | bytes 786440 | tf_op jit(solution)/shard_map/ppermute | solution.py:39
  240.9 25.8 %collective-permute-start.26 = (bf16[1024,512]{1,0:T(8,128)(2,1)}, bf16[1024,512]{1,0:T(8,128)(2,1)}, u32[]{:S(2)}, u32[]{:S(2)}) collective-permute-start(bf16[1024,512]{1,0:T(8,128)(2,1)} %fusion.187), channel_id=1, source_target_pairs={{0,2},{1,3},{2,0},{3,1},{4,6},{5,7},{6,4},{7,5},{8,10},{9,11},{10,... | collective-permute-start | bytes 3145736 | tf_op jit(solution)/shard_map/ppermute | solution.py:39
  241.4 25.2 %collective-permute-start.24 = (bf16[1024,512]{1,0:T(8,128)(2,1)}, bf16[1024,512]{1,0:T(8,128)(2,1)}, u32[]{:S(2)}, u32[]{:S(2)}) collective-permute-start(bf16[1024,512]{1,0:T(8,128)(2,1)} %fusion.187), channel_id=1, source_target_pairs={{0,1},{1,0},{2,3},{3,2},{4,5},{5,4},{6,7},{7,6},{8,9},{9,8},{10,11... | collective-permute-start | bytes 3145736 | tf_op jit(solution)/shard_map/ppermute | solution.py:39
  272.2 134.8 %collective-permute-start.25 = (bf16[1024,512]{1,0:T(8,128)(2,1)}, bf16[1024,512]{1,0:T(8,128)(2,1)S(1)}, u32[]{:S(2)}, u32[]{:S(2)}) collective-permute-start(bf16[1024,512]{1,0:T(8,128)(2,1)} %fusion.145), channel_id=1, source_target_pairs={{0,1},{1,0},{2,3},{3,2},{4,5},{5,4},{6,7},{7,6},{8,9},{9,8},{10,11... | collective-permute-start | bytes 3145736 | tf_op jit(solution)/shard_map/ppermute | solution.py:39
  280.5 72.0 %collective-permute-start.28 = (bf16[1024,512]{1,0:T(8,128)(2,1)}, bf16[1024,512]{1,0:T(8,128)(2,1)}, u32[]{:S(2)}, u32[]{:S(2)}) collective-permute-start(bf16[1024,512]{1,0:T(8,128)(2,1)} %fusion.146), channel_id=1, source_target_pairs={{0,1},{1,0},{2,3},{3,2},{4,5},{5,4},{6,7},{7,6},{8,9},{9,8},{10,11... | collective-permute-start | bytes 3145736 | tf_op jit(solution)/shard_map/ppermute | solution.py:39
  296.7 21.5 %collective-permute-start.87 = (bf16[256,1024]{1,0:T(8,128)(2,1)S(1)}, bf16[256,1024]{1,0:T(8,128)(2,1)S(1)}, u32[]{:S(2)}, u32[]{:S(2)}) collective-permute-start(bf16[256,1024]{1,0:T(8,128)(2,1)S(1)} %constant_dynamic-slice_fusion.33), channel_id=1, source_target_pairs={{0,8},{4,12},{8,0},{12,4},{16,24},{20,28},{24,16},{28,20},{1,9},{5... | collective-permute-start | bytes 1572872 | tf_op jit(solution)/shard_map/ppermute | solution.py:39
  318.8 20.9 %collective-permute-start.82 = (bf16[128,1024]{1,0:T(8,128)(2,1)S(1)}, bf16[128,1024]{1,0:T(8,128)(2,1)S(1)}, u32[]{:S(2)}, u32[]{:S(2)}) collective-permute-start(bf16[128,1024]{1,0:T(8,128)(2,1)S(1)} %constant_dynamic-slice_fusion.1), channel_id=1, source_target_pairs={{0,8},{4,12},{8,0},{12,4},{16,24},{20,28},{24,16},{28,20},{1,9},{5... | collective-permute-start | bytes 786440 | tf_op jit(solution)/shard_map/ppermute | solution.py:39
  355.2 19.7 %collective-permute-start.79 = (bf16[128,1024]{1,0:T(8,128)(2,1)S(1)}, bf16[128,1024]{1,0:T(8,128)(2,1)S(1)}, u32[]{:S(2)}, u32[]{:S(2)}) collective-permute-start(bf16[128,1024]{1,0:T(8,128)(2,1)S(1)} %constant_dynamic-update-slice_fusion.5), channel_id=1, source_target_pairs={{0,16},{4,20},{8,24},{12,28},{16,0},{20,4},{24,8},{28,12},{1,17},{... | collective-permute-start | bytes 786440 | tf_op jit(solution)/shard_map/ppermute | solution.py:39
  358.5 21.1 %collective-permute-start.91 = (bf16[128,1024]{1,0:T(8,128)(2,1)S(1)}, bf16[128,1024]{1,0:T(8,128)(2,1)S(1)}, u32[]{:S(2)}, u32[]{:S(2)}) collective-permute-start(bf16[128,1024]{1,0:T(8,128)(2,1)S(1)} %constant_dynamic-update-slice_fusion.22), channel_id=1, source_target_pairs={{0,16},{4,20},{8,24},{12,28},{16,0},{20,4},{24,8},{28,12},{1,17},{... | collective-permute-start | bytes 786440 | tf_op jit(solution)/shard_map/ppermute | solution.py:39
  379.6 22.3 %collective-permute-start.92 = (bf16[256,1024]{1,0:T(8,128)(2,1)S(1)}, bf16[256,1024]{1,0:T(8,128)(2,1)S(1)}, u32[]{:S(2)}, u32[]{:S(2)}) collective-permute-start(bf16[256,1024]{1,0:T(8,128)(2,1)S(1)} %constant_dynamic-update-slice_fusion.21), channel_id=1, source_target_pairs={{0,8},{4,12},{8,0},{12,4},{16,24},{20,28},{24,16},{28,20},{1,9},{5... | collective-permute-start | bytes 1572872 | tf_op jit(solution)/shard_map/ppermute | solution.py:39
  382.4 19.6 %collective-permute-start.86 = (bf16[256,1024]{1,0:T(8,128)(2,1)S(1)}, bf16[256,1024]{1,0:T(8,128)(2,1)S(1)}, u32[]{:S(2)}, u32[]{:S(2)}) collective-permute-start(bf16[256,1024]{1,0:T(8,128)(2,1)S(1)} %constant_dynamic-update-slice_fusion.1), channel_id=1, source_target_pairs={{0,4},{4,0},{8,12},{12,8},{16,20},{20,16},{24,28},{28,24},{1,5},{5... | collective-permute-start | bytes 1572872 | tf_op jit(solution)/shard_map/ppermute | solution.py:39
  417.1 113.9 %collective-permute-start.18 = (bf16[256,512]{1,0:T(8,128)(2,1)}, bf16[256,512]{1,0:T(8,128)(2,1)}, u32[]{:S(2)}, u32[]{:S(2)}) collective-permute-start(bf16[256,512]{1,0:T(8,128)(2,1)} %get-tuple-element.71), channel_id=1, source_target_pairs={{0,1},{1,0},{2,3},{3,2},{4,5},{5,4},{6,7},{7,6},{8,9},{9,8},{10,11... | collective-permute-start | bytes 786440 | tf_op jit(solution)/shard_map/ppermute | solution.py:39
  417.1 118.9 %collective-permute-start.19 = (bf16[256,512]{1,0:T(8,128)(2,1)}, bf16[256,512]{1,0:T(8,128)(2,1)}, u32[]{:S(2)}, u32[]{:S(2)}) collective-permute-start(bf16[256,512]{1,0:T(8,128)(2,1)} %get-tuple-element.70), channel_id=1, source_target_pairs={{0,2},{1,3},{2,0},{3,1},{4,6},{5,7},{6,4},{7,5},{8,10},{9,11},{10,... | collective-permute-start | bytes 786440 | tf_op jit(solution)/shard_map/ppermute | solution.py:39
  430.0 109.8 %collective-permute-start.20 = (bf16[256,512]{1,0:T(8,128)(2,1)}, bf16[256,512]{1,0:T(8,128)(2,1)}, u32[]{:S(2)}, u32[]{:S(2)}) collective-permute-start(bf16[256,512]{1,0:T(8,128)(2,1)} %get-tuple-element.69), channel_id=1, source_target_pairs={{0,3},{1,2},{2,1},{3,0},{4,7},{5,6},{6,5},{7,4},{8,11},{9,10},{10,... | collective-permute-start | bytes 786440 | tf_op jit(solution)/shard_map/ppermute | solution.py:39
  437.6 110.7 %collective-permute-start.55 = (bf16[256,1024]{1,0:T(8,128)(2,1)}, bf16[256,1024]{1,0:T(8,128)(2,1)}, u32[]{:S(2)}, u32[]{:S(2)}) collective-permute-start(bf16[256,1024]{1,0:T(8,128)(2,1)} %get-tuple-element.54), channel_id=1, source_target_pairs={{0,1},{1,0},{2,3},{3,2},{4,5},{5,4},{6,7},{7,6},{8,9},{9,8},{10,11... | collective-permute-start | bytes 1572872 | tf_op jit(solution)/shard_map/ppermute | solution.py:39
  523.3 22.4 %collective-permute-start.48 = (bf16[768,256]{1,0:T(8,128)(2,1)}, bf16[768,256]{1,0:T(8,128)(2,1)S(1)}, u32[]{:S(2)}, u32[]{:S(2)}) collective-permute-start(bf16[768,256]{1,0:T(8,128)(2,1)} %get-tuple-element.84), channel_id=1, source_target_pairs={{0,8},{4,12},{8,0},{12,4},{16,24},{20,28},{24,16},{28,20},{1,9},{5... | collective-permute-start | bytes 1179656 | tf_op jit(solution)/shard_map/ppermute | solution.py:39
  539.8 50.8 %collective-permute-start.54 = (bf16[256,1024]{1,0:T(8,128)(2,1)S(1)}, bf16[256,1024]{1,0:T(8,128)(2,1)S(1)}, u32[]{:S(2)}, u32[]{:S(2)}) collective-permute-start(bf16[256,1024]{1,0:T(8,128)(2,1)S(1)} %copy-done.39), channel_id=1, source_target_pairs={{0,1},{1,0},{2,3},{3,2},{4,5},{5,4},{6,7},{7,6},{8,9},{9,8},{10,11... | collective-permute-start | bytes 1572872 | tf_op jit(solution)/shard_map/ppermute | solution.py:39
  544.5 74.6 %collective-permute-start.34 = (bf16[256,2048]{1,0:T(8,128)(2,1)}, bf16[256,2048]{1,0:T(8,128)(2,1)S(1)}, u32[]{:S(2)}, u32[]{:S(2)}) collective-permute-start(bf16[256,2048]{1,0:T(8,128)(2,1)} %get-tuple-element.58), channel_id=1, source_target_pairs={{0,1},{1,0},{2,3},{3,2},{4,5},{5,4},{6,7},{7,6},{8,9},{9,8},{10,11... | collective-permute-start | bytes 3145736 | tf_op jit(solution)/shard_map/ppermute | solution.py:39
  545.7 93.3 %collective-permute-start.33 = (bf16[256,2048]{1,0:T(8,128)(2,1)}, bf16[256,2048]{1,0:T(8,128)(2,1)S(1)}, u32[]{:S(2)}, u32[]{:S(2)}) collective-permute-start(bf16[256,2048]{1,0:T(8,128)(2,1)} %get-tuple-element.56), channel_id=1, source_target_pairs={{0,1},{1,0},{2,3},{3,2},{4,5},{5,4},{6,7},{7,6},{8,9},{9,8},{10,11... | collective-permute-start | bytes 3145736 | tf_op jit(solution)/shard_map/ppermute | solution.py:39
  549.6 41.1 %collective-permute-start.56 = (bf16[256,1024]{1,0:T(8,128)(2,1)S(1)}, bf16[256,1024]{1,0:T(8,128)(2,1)S(1)}, u32[]{:S(2)}, u32[]{:S(2)}) collective-permute-start(bf16[256,1024]{1,0:T(8,128)(2,1)S(1)} %add_convert_fusion.8), channel_id=1, source_target_pairs={{0,2},{1,3},{2,0},{3,1},{4,6},{5,7},{6,4},{7,5},{8,10},{9,11},{10,... | collective-permute-start | bytes 1572872 | tf_op jit(solution)/shard_map/ppermute | solution.py:39
  605.5 26.4 %collective-permute-start.53 = (bf16[768,256]{1,0:T(8,128)(2,1)S(1)}, bf16[768,256]{1,0:T(8,128)(2,1)S(1)}, u32[]{:S(2)}, u32[]{:S(2)}) collective-permute-start(bf16[768,256]{1,0:T(8,128)(2,1)S(1)} %constant_dynamic-update-slice_fusion.16), channel_id=1, source_target_pairs={{0,8},{4,12},{8,0},{12,4},{16,24},{20,28},{24,16},{28,20},{1,9},{5... | collective-permute-start | bytes 1179656 | tf_op jit(solution)/shard_map/ppermute | solution.py:39
  619.5 19.5 %collective-permute-start.35 = (bf16[256,2048]{1,0:T(8,128)(2,1)S(1)}, bf16[256,2048]{1,0:T(8,128)(2,1)S(1)}, u32[]{:S(2)}, u32[]{:S(2)}) collective-permute-start(bf16[256,2048]{1,0:T(8,128)(2,1)S(1)} %add_convert_fusion.1), channel_id=1, source_target_pairs={{0,2},{1,3},{2,0},{3,1},{4,6},{5,7},{6,4},{7,5},{8,10},{9,11},{10,... | collective-permute-start | bytes 3145736 | tf_op jit(solution)/shard_map/ppermute | solution.py:39
  (125 other events, 1349.4 us)

commit v2 on v1

v2 whole, which is shorter than its diff:
```python
import math

import jax
import jax.numpy as jnp
from jax import lax
from jax.experimental import pallas as pl
from jax.experimental.pallas import tpu as pltpu
from jax.sharding import PartitionSpec as P

D = 1024
HEADS = 16
HEAD = 64
SEQ_LEN = 2048

EPS = 1e-05
BIG = 1e30
Q_BLOCK = 512
K_CHUNK = 512
K_CHUNK_BACK = 256
VMEM_LIMIT = 56 * 1024 * 1024

F32 = jnp.float32
BF16 = jnp.bfloat16


def lead_dot(left, right):
    return lax.dot_general(left, right, (((0,), (0,)), ((), ())), preferred_element_type=F32)


def tail_dot(left, right):
    return lax.dot_general(left, right, (((1,), (1,)), ((), ())), preferred_element_type=F32)


def dot(left, right):
    return jnp.dot(left, right, preferred_element_type=F32)


def swap(piece, axis, mask):
    count = lax.axis_size(axis)
    return lax.ppermute(piece, axis, [(i, i ^ mask) for i in range(count)])


def bits_of(axis):
    count, found, bit = lax.axis_size(axis), [], 1
    while bit < count:
        found.append(bit)
        bit *= 2
    return found


def gather_slots(slots, axis, bits=None):
    slots = dict(slots)
    for bit in reversed(bits or bits_of(axis)):
        for slot in sorted(slots):
            slots[slot | bit] = swap(slots[slot], axis, bit)
    return slots


def slot_order(count):
    kept = [0]
    bit = count // 2
    while bit:
        kept = [slot for slot in kept] + [slot | bit for slot in kept]
        bit //= 2
    return kept


def scatter_stack(stack, axis, wire=BF16, late=None):
    for bit in bits_of(axis):
        half = stack.shape[0] // 2
        sent = stack[half:].astype(wire)
        if late is not None and bit > 1:
            sent = sent + late
        moved = swap(sent, axis, bit)
        stack = stack[:half].astype(F32) + moved.astype(F32)
    return stack


def gather_apply(own_piece, axis, apply):
    bits = bits_of(axis)
    half = own_piece.shape[1] // 2
    slots = {0: own_piece}
    for bit in reversed(bits[1:]):
        for slot in sorted(slots):
            slots[slot | bit] = swap(slots[slot], axis, bit)
    far = [slot for slot in sorted(slots) if slot]
    beside = swap(own_piece, axis, 1)
    term = apply(0, own_piece)
    term_beside = apply(2 * half, beside)
    got_beside = swap(term_beside, axis, 1)
    after, at, sums = term_beside[0, 0] * 0, 4 * half, []
    for slot in far:
        slots[slot | 1] = swap(slots[slot] + after, axis, 1)
    names = [slot for slot in sorted(slots) if slot > 1]
    done = None
    for i in range(2):
        columns = slice(i * half, (i + 1) * half)
        last = apply(at, jnp.concatenate([slots[slot][:, columns] for slot in names], axis=1))
        at += half * len(names)
        terms = {slot: last[:, k * half : (k + 1) * half] for k, slot in enumerate(names)}
        for slot in far:
            sent = terms.pop(slot | 1)
            if done is not None:
                sent = sent + done
            terms[slot] = terms[slot].astype(F32) + swap(sent, axis, 1).astype(F32)
        terms[0] = term[:, columns].astype(F32) + got_beside[:, columns].astype(F32)
        for bit in bits[1:]:
            for slot in sorted(terms, reverse=True):
                if slot & bit:
                    got = swap(terms.pop(slot).astype(BF16), axis, bit)
                    done = got[0, 0] * 0
                    terms[slot ^ bit] = terms[slot ^ bit] + got.astype(F32)
        sums.append(terms[0])
    return jnp.concatenate(sums, axis=1)


def place(slots, own, dim):
    count, width = len(slots), slots[0].shape[dim]
    shape = list(slots[0].shape)
    shape[dim] = width * count
    whole = jnp.zeros(shape, slots[0].dtype)
    for slot in sorted(slots):
        whole = lax.dynamic_update_slice_in_dim(whole, slots[slot], (own ^ slot) * width, dim)
    return whole


def cut(whole, own, slot, count, dim):
    width = whole.shape[dim] // count
    return lax.dynamic_slice_in_dim(whole, (own ^ slot) * width, width, dim)


def exchange(whole, own, axis, dim):
    count = lax.axis_size(axis)
    return {
        slot: swap(cut(whole, own, slot, count, dim), axis, slot)
        if slot
        else cut(whole, own, 0, count, dim)
        for slot in range(count)
    }


def sum_weights(piece, axis):
    index = lax.axis_index(axis)
    bits = bits_of(axis)
    groups = []
    for group in (bits[: len(bits) // 2], bits[len(bits) // 2 :]):
        masks = [0]
        for bit in group:
            masks = masks + [mask | bit for mask in masks]
        groups.append((masks, (index // (group or [1])[0]) % len(masks)))
    rows = piece.shape[0] * 2 // 3
    pieces = [piece[:rows], piece[rows:]]
    for phase in range(2):
        fresh = []
        for part in range(2):
            masks, spot = groups[phase ^ part]
            count = len(masks)
            total = cut(pieces[part], spot, 0, count, 0).astype(F32)
            for r in range(1, count):
                total = total + swap(cut(pieces[part], spot, r, count, 0), axis, masks[r]).astype(F32)
            fresh.append(total)
        zero = [(total[0, 0] * 0).astype(piece.dtype) for total in fresh]
        if phase == 0:
            begun = zero[0] + zero[1]
        pieces = [fresh[part].astype(piece.dtype) + zero[1 - part] for part in range(2)]
    for phase in (1, 0):
        fresh = []
        for part in range(2):
            masks, spot = groups[phase ^ part]
            fresh.append(
                place({r: swap(pieces[part], axis, mask) if mask else pieces[part] for r, mask in enumerate(masks)}, spot, 0)
            )
        if phase:
            zero = [whole[0, 0] * 0 for whole in fresh]
            pieces = [fresh[part] + zero[1 - part] for part in range(2)]
        else:
            pieces = fresh
    return pieces, begun


def seg_codes(segment_ids):
    digits = jnp.arange(16, dtype=jnp.int32)[:, None]
    low = (segment_ids[None, :] & 15) == digits
    high = ((segment_ids[None, :] >> 4) & 15) == digits
    same = jnp.concatenate([low, high], axis=0)
    keys = same.astype(BF16)
    queries = jnp.where(same, 0.0, -BIG).astype(BF16)
    return keys, queries


def key_ranges(segment_ids, seq_count, chunk):
    rows = segment_ids.reshape(seq_count, 1, SEQ_LEN)
    blocks = segment_ids.reshape(seq_count, SEQ_LEN // Q_BLOCK, Q_BLOCK)
    first = jnp.sum((rows < blocks[:, :, :1]).astype(jnp.int32), axis=-1)
    last = jnp.sum((rows <= blocks[:, :, -1:]).astype(jnp.int32), axis=-1)
    return (first // chunk).reshape(-1), ((last + chunk - 1) // chunk).reshape(-1)


def three_parts(row):
    lines = lax.broadcasted_iota(jnp.int32, (16, row.shape[1]), 0)
    first = row.astype(BF16).astype(F32)
    second = (row - first).astype(BF16).astype(F32)
    third = row - first - second
    spread = jnp.where(
        lines == 0, first, jnp.where(lines == 1, second, jnp.where(lines == 2, third, 0.0))
    )
    return spread.astype(BF16)


def attend_kernel(heads, from_ref, to_ref, q_ref, k_ref, v_ref, qc_ref, kc_ref, o_ref, lse_ref, kt, va, top, acc):
    seq, block = pl.program_id(0), pl.program_id(1)
    spot = seq * pl.num_programs(1) + block

    @pl.when(block == 0)
    def _():
        codes = kc_ref[...].astype(F32)
        for h in range(heads):
            rows = slice(h * HEAD, (h + 1) * HEAD)
            lines = lax.broadcasted_iota(jnp.int32, (16, SEQ_LEN), 0)
            ones = jnp.where(lines < 3, 1.0, 0.0).astype(F32)
            whole = jnp.concatenate([k_ref[rows, :].astype(F32), codes, ones, jnp.zeros_like(ones)], axis=0)
            kt[h] = whole.T.astype(BF16)
            va[h] = jnp.concatenate(
                [v_ref[rows, :], jnp.where(lines == 0, 1.0, 0.0).astype(BF16)], axis=0
            )

    top[...] = jnp.full_like(top, -BIG)
    acc[...] = jnp.zeros_like(acc)
    queries = []
    for h in range(heads):
        scaled = (q_ref[h * HEAD : (h + 1) * HEAD, :].astype(F32) * (1.0 / math.sqrt(HEAD))).astype(BF16)
        queries.append(
            jnp.concatenate([scaled, qc_ref[...], jnp.zeros((32, Q_BLOCK), BF16)], axis=0)
        )

    def highest(chunk, carry):
        at = pl.multiple_of(chunk * K_CHUNK, K_CHUNK)
        for h in range(heads):
            scores = dot(kt[h, pl.ds(at, K_CHUNK), :], queries[h])
            top[h] = jnp.maximum(top[h], jnp.max(scores.reshape(K_CHUNK // 8, 8, Q_BLOCK), axis=0))
        return carry

    lax.fori_loop(from_ref[spot], to_ref[spot], highest, 0)
    peaks, shifted = [], []
    blank = jnp.zeros((16, Q_BLOCK), BF16)
    for h in range(heads):
        peaks.append(jnp.max(top[h], axis=0, keepdims=True))
        shifted.append(
            jnp.concatenate([queries[h][:96], three_parts(-peaks[h]), blank], axis=0)
        )

    def step(chunk, carry):
        at = pl.multiple_of(chunk * K_CHUNK, K_CHUNK)
        moved = [dot(kt[h, pl.ds(at, K_CHUNK), :], shifted[h]) for h in range(heads)]
        raised = [jnp.exp(scores).astype(BF16) for scores in moved]
        for h in range(heads):
            acc[h] += dot(va[h, :, pl.ds(at, K_CHUNK)], raised[h])
        return carry

    lax.fori_loop(from_ref[spot], to_ref[spot], step, 0)
    for h in range(heads):
        total = acc[h, HEAD : HEAD + 1, :]
        o_ref[h * HEAD : (h + 1) * HEAD, :] = (acc[h, :HEAD, :] / total).astype(BF16)
        lse_ref[0, h : h + 1, :] = peaks[h] + jnp.log(total)


def attend(queries, keys, values, codes_q, codes_k, ranges, seq_count):
    width, length = queries.shape
    heads = width // HEAD
    blocks = SEQ_LEN // Q_BLOCK
    by_block = lambda s, b, *_: (0, s * blocks + b)
    by_seq = lambda s, b, *_: (0, s)
    spec = pltpu.PrefetchScalarGridSpec(
        num_scalar_prefetch=2,
        grid=(seq_count, blocks),
        in_specs=[
            pl.BlockSpec((width, Q_BLOCK), by_block),
            pl.BlockSpec((width, SEQ_LEN), by_seq),
            pl.BlockSpec((width, SEQ_LEN), by_seq),
            pl.BlockSpec((32, Q_BLOCK), by_block),
            pl.BlockSpec((32, SEQ_LEN), by_seq),
        ],
        out_specs=[
            pl.BlockSpec((width, Q_BLOCK), by_block),
            pl.BlockSpec((1, heads, Q_BLOCK), lambda s, b, *_: (0, 0, s * blocks + b)),
        ],
        scratch_shapes=[
            pltpu.VMEM((heads, SEQ_LEN, 128), BF16),
            pltpu.VMEM((heads, HEAD + 16, SEQ_LEN), BF16),
            pltpu.VMEM((heads, 8, Q_BLOCK), F32),
            pltpu.VMEM((heads, HEAD + 16, Q_BLOCK), F32),
        ],
    )
    area = length * SEQ_LEN * heads
    return pl.pallas_call(
        lambda *refs: attend_kernel(heads, *refs),
        grid_spec=spec,
        out_shape=[
            jax.ShapeDtypeStruct((width, length), BF16),
            jax.ShapeDtypeStruct((1, heads, length), F32),
        ],
        compiler_params=pltpu.CompilerParams(
            dimension_semantics=("arbitrary", "arbitrary"), vmem_limit_bytes=VMEM_LIMIT
        ),
        cost_estimate=pl.CostEstimate(flops=12 * HEAD * area, bytes_accessed=8 * width * length, transcendentals=area),
        name="attend",
    )(*ranges, queries, keys, values, codes_q, codes_k)


def attend_back_kernel(
    heads, from_ref, to_ref, q_ref, o_ref, do_ref, lse_ref, k_ref, v_ref, qc_ref, kc_ref, out_ref, kt, vt, acc, dq_acc
):
    seq, block = pl.program_id(0), pl.program_id(1)
    spot = seq * pl.num_programs(1) + block

    @pl.when(block == 0)
    def _():
        codes = kc_ref[...].astype(F32)
        lines = lax.broadcasted_iota(jnp.int32, (16, SEQ_LEN), 0)
        ones = jnp.where(lines < 3, 1.0, 0.0).astype(F32)
        blank = jnp.zeros((16, SEQ_LEN), F32)
        for h in range(heads):
            rows = slice(h * HEAD, (h + 1) * HEAD)
            kt[h] = jnp.concatenate([k_ref[rows, :].astype(F32), codes, ones, blank], axis=0).T.astype(BF16)
            vt[h] = jnp.concatenate([v_ref[rows, :].astype(F32), ones, blank, blank, blank], axis=0).T.astype(BF16)
        acc[...] = jnp.zeros_like(acc)

    dq_acc[...] = jnp.zeros_like(dq_acc)
    lanes = lax.broadcasted_iota(jnp.int32, (Q_BLOCK, 128), 1)
    blank = jnp.zeros((16, Q_BLOCK), BF16)

    queries, grads, both = [], [], []
    for h in range(heads):
        rows = slice(h * HEAD, (h + 1) * HEAD)
        scaled = q_ref[rows, :].astype(F32) * (1.0 / math.sqrt(HEAD))
        grad = do_ref[rows, :].astype(F32)
        centre = jnp.sum(grad * o_ref[rows, :].astype(F32), axis=0, keepdims=True)
        queries.append(
            jnp.concatenate([scaled.astype(BF16), qc_ref[...], three_parts(-lse_ref[0, h : h + 1, :]), blank], axis=0)
        )
        grads.append(jnp.concatenate([do_ref[rows, :], three_parts(-centre), blank, blank, blank], axis=0))
        turned = jnp.concatenate([grad, scaled], axis=0).T
        both.append(
            jnp.concatenate(
                [jnp.where(lanes < HEAD, turned, 0.0), jnp.where(lanes < HEAD, 0.0, turned)], axis=0
            ).astype(BF16)
        )

    def step(chunk, carry):
        span = pl.ds(pl.multiple_of(chunk * K_CHUNK_BACK, K_CHUNK_BACK), K_CHUNK_BACK)
        for h in range(heads):
            softened = jnp.exp(dot(kt[h, span, :], queries[h]))
            shifted = dot(vt[h, span, :], grads[h])
            score_grad = (softened * shifted).astype(BF16)
            pair = jnp.concatenate([softened.astype(BF16), score_grad], axis=1)
            acc[h, span, :] += dot(pair, both[h])
            dq_acc[h] += dot(k_ref[h * HEAD : (h + 1) * HEAD, span], score_grad)
        return carry

    lax.fori_loop(from_ref[spot], to_ref[spot], step, 0)
    query_rows = [None] * heads
    for h in range(heads):
        query_rows[h] = dq_acc[h] * (1.0 / math.sqrt(HEAD))
    own_rows = pl.ds(pl.multiple_of(block * Q_BLOCK, Q_BLOCK), Q_BLOCK)
    out_ref[own_rows, 2 * heads * HEAD :] = jnp.concatenate(query_rows, axis=0).T.astype(BF16)

    @pl.when(block == pl.num_programs(1) - 1)
    def _():
        out_ref[:, : heads * HEAD] = jnp.concatenate(
            [acc[h, :, :HEAD] for h in range(heads)], axis=1
        ).astype(BF16)
        out_ref[:, heads * HEAD : 2 * heads * HEAD] = jnp.concatenate(
            [acc[h, :, HEAD:] for h in range(heads)], axis=1
        ).astype(BF16)


def attend_back(queries, context, grads, log_totals, keys, values, codes_q, codes_k, ranges, seq_count):
    width, length = queries.shape
    heads = width // HEAD
    blocks = SEQ_LEN // Q_BLOCK
    by_block = lambda s, b, *_: (0, s * blocks + b)
    by_seq = lambda s, b, *_: (0, s)
    spec = pltpu.PrefetchScalarGridSpec(
        num_scalar_prefetch=2,
        grid=(seq_count, blocks),
        in_specs=[
            pl.BlockSpec((width, Q_BLOCK), by_block),
            pl.BlockSpec((width, Q_BLOCK), by_block),
            pl.BlockSpec((width, Q_BLOCK), by_block),
            pl.BlockSpec((1, heads, Q_BLOCK), lambda s, b, *_: (0, 0, s * blocks + b)),
            pl.BlockSpec((width, SEQ_LEN), by_seq),
            pl.BlockSpec((width, SEQ_LEN), by_seq),
            pl.BlockSpec((32, Q_BLOCK), by_block),
            pl.BlockSpec((32, SEQ_LEN), by_seq),
        ],
        out_specs=pl.BlockSpec((SEQ_LEN, 3 * width), lambda s, b, *_: (s, 0)),
        scratch_shapes=[
            pltpu.VMEM((heads, SEQ_LEN, 128), BF16),
            pltpu.VMEM((heads, SEQ_LEN, 128), BF16),
            pltpu.VMEM((heads, SEQ_LEN, 128), F32),
            pltpu.VMEM((heads, HEAD, Q_BLOCK), F32),
        ],
    )
    area = length * SEQ_LEN * heads
    return pl.pallas_call(
        lambda *refs: attend_back_kernel(heads, *refs),
        grid_spec=spec,
        out_shape=jax.ShapeDtypeStruct((length, 3 * width), BF16),
        compiler_params=pltpu.CompilerParams(
            dimension_semantics=("arbitrary", "arbitrary"), vmem_limit_bytes=VMEM_LIMIT
        ),
        cost_estimate=pl.CostEstimate(flops=30 * HEAD * area, bytes_accessed=14 * width * length, transcendentals=area),
        name="attend_back",
    )(*ranges, queries, context, grads, log_totals, keys, values, codes_q, codes_k)


TOKEN_BLOCK = 256


def feed_kernel(y_ref, up_ref, bias_ref, down_ref, *refs):
    y_out, g_ref, slope_ref, part_ref = refs[-4:]
    hidden = up_ref.shape[0]
    piece = min(256, hidden)
    total = None
    y_out[...] = y_ref[...]
    for at in range(0, hidden, piece):
        rows = slice(at, at + piece)
        upward = dot(up_ref[rows, :], y_ref[...]) + bias_ref[rows, :]
        flat = (1.0 + lax.erf(upward * (1.0 / math.sqrt(2.0)))) * 0.5
        slope = flat + upward * jnp.exp(upward * upward * -0.5) * (1.0 / math.sqrt(2.0 * math.pi))
        active = (upward * flat).astype(BF16)
        g_ref[rows, :] = active
        slope_ref[rows, :] = slope.astype(BF16)
        term = dot(down_ref[:, rows], active)
        total = term if total is None else total + term
    part_ref[...] = total.astype(part_ref.dtype)


def feed(at, total, kept, first_low, up_turned, bias_up, down_turned):
    tokens = first_low.shape[1]
    hidden = up_turned.shape[0]
    blocks = tokens // TOKEN_BLOCK
    by_token = lambda t: (0, t)
    in_whole = lambda t: (0, at // TOKEN_BLOCK + t)
    whole = lambda t: (0, 0)
    *kept, part = pl.pallas_call(
        feed_kernel,
        grid=(blocks,),
        in_specs=[
            pl.BlockSpec((D, TOKEN_BLOCK), by_token),
            pl.BlockSpec((hidden, D), whole),
            pl.BlockSpec((hidden, 1), whole),
            pl.BlockSpec((D, hidden), whole),
        ]
        + [pl.BlockSpec(memory_space=pl.ANY)] * len(kept),
        out_specs=[
            pl.BlockSpec((D, TOKEN_BLOCK), in_whole),
            pl.BlockSpec((hidden, TOKEN_BLOCK), in_whole),
            pl.BlockSpec((hidden, TOKEN_BLOCK), in_whole),
            pl.BlockSpec((D, TOKEN_BLOCK), by_token),
        ],
        out_shape=[
            jax.ShapeDtypeStruct((D, total), BF16),
            jax.ShapeDtypeStruct((hidden, total), BF16),
            jax.ShapeDtypeStruct((hidden, total), BF16),
            jax.ShapeDtypeStruct((D, tokens), BF16),
        ],
        input_output_aliases={4 + i: i for i in range(len(kept))},
        compiler_params=pltpu.CompilerParams(
            dimension_semantics=("arbitrary",), vmem_limit_bytes=VMEM_LIMIT
        ),
        cost_estimate=pl.CostEstimate(
            flops=4 * D * hidden * tokens, bytes_accessed=4 * D * hidden + 8 * D * tokens, transcendentals=2 * hidden * tokens
        ),
        name="feed",
    )(first_low, up_turned, bias_up, down_turned, *kept)
    return kept, part


def feed_back_kernel(m_ref, slope_ref, down_ref, up_ref, *refs):
    m_out, du_ref, part_ref = refs[-3:]
    hidden = down_ref.shape[0]
    piece = min(256, hidden)
    total = None
    m_out[...] = m_ref[...]
    for at in range(0, hidden, piece):
        rows = slice(at, at + piece)
        grad = (dot(down_ref[rows, :], m_ref[...]) * slope_ref[rows, :].astype(F32)).astype(BF16)
        du_ref[rows, :] = grad
        term = dot(up_ref[:, rows], grad)
        total = term if total is None else total + term
    part_ref[...] = total.astype(part_ref.dtype)


def feed_back(at, total, kept, down_low, slope, w_down, w_up):
    tokens = down_low.shape[1]
    hidden = w_down.shape[0]
    blocks = tokens // TOKEN_BLOCK
    by_token = lambda t: (0, t)
    in_whole = lambda t: (0, at // TOKEN_BLOCK + t)
    whole = lambda t: (0, 0)
    *kept, part = pl.pallas_call(
        feed_back_kernel,
        grid=(blocks,),
        in_specs=[
            pl.BlockSpec((D, TOKEN_BLOCK), by_token),
            pl.BlockSpec((hidden, TOKEN_BLOCK), in_whole),
            pl.BlockSpec((hidden, D), whole),
            pl.BlockSpec((D, hidden), whole),
        ]
        + [pl.BlockSpec(memory_space=pl.ANY)] * len(kept),
        out_specs=[
            pl.BlockSpec((D, TOKEN_BLOCK), in_whole),
            pl.BlockSpec((hidden, TOKEN_BLOCK), in_whole),
            pl.BlockSpec((D, TOKEN_BLOCK), by_token),
        ],
        out_shape=[
            jax.ShapeDtypeStruct((D, total), BF16),
            jax.ShapeDtypeStruct((hidden, total), BF16),
            jax.ShapeDtypeStruct((D, tokens), BF16),
        ],
        input_output_aliases={4 + i: i for i in range(len(kept))},
        compiler_params=pltpu.CompilerParams(
            dimension_semantics=("arbitrary",), vmem_limit_bytes=VMEM_LIMIT
        ),
        cost_estimate=pl.CostEstimate(
            flops=4 * D * hidden * tokens, bytes_accessed=4 * D * hidden + 8 * D * tokens, transcendentals=0
        ),
        name="feed_back",
    )(down_low, slope, w_down, w_up, *kept)
    return kept, part


def norm_rows(values, norm_gain, norm_shift):
    centre = values - jnp.mean(values, axis=0, keepdims=True)
    inverse = lax.rsqrt(jnp.mean(centre * centre, axis=0, keepdims=True) + EPS)
    normed = centre * inverse
    return (normed * norm_gain[:, None] + norm_shift[:, None], normed, inverse)


def norm_back(grad_rows, normed, inverse, norm_gain):
    scaled = grad_rows * norm_gain[:, None]
    return inverse * (
        scaled
        - jnp.mean(scaled, axis=0, keepdims=True)
        - normed * jnp.mean(scaled * normed, axis=0, keepdims=True)
    )


def body(
    hidden_in,
    segment_ids,
    w_query,
    b_query,
    w_key,
    w_value,
    b_value,
    w_out,
    b_out,
    gain_one,
    shift_one,
    w_up,
    b_up,
    w_down,
    b_down,
    gain_two,
    shift_two,
    cotangent,
):
    parts = lax.axis_size("mp")
    own = lax.axis_index("mp")
    width, length = hidden_in.shape
    seq_count = length // SEQ_LEN
    own_len = length // parts
    own_heads = width // HEAD

    input_slots = gather_slots({0: hidden_in}, "mp")
    inputs = place(input_slots, own, 0)
    after = input_slots[parts // 2][0, 0] * 0
    vectors = jnp.stack([b_out, gain_one, shift_one, b_down, gain_two, shift_two])
    vectors = place(gather_slots({0: vectors}, "mp"), own, 1).astype(F32)
    bias_out, gain_first, shift_first, bias_down, gain_second, shift_second = [vectors[i] for i in range(6)]
    out_slots = gather_slots({0: w_out + after}, "mp", bits_of("mp")[1:])
    cot_own = place(exchange(cotangent, own + after.astype(jnp.int32), "mp", 1), own, 0)
    up_turned, down_turned = w_up.T, w_down.T
    order = slot_order(parts)

    w_three = jnp.concatenate([w_value, w_key, w_query], axis=1)
    biases = jnp.concatenate([b_value, jnp.zeros_like(b_query), b_query]).astype(F32)[:, None]
    projected = (dot(w_three.T, inputs) + biases).astype(BF16)
    values, keys, queries = projected[:width], projected[width : 2 * width], projected[2 * width :]
    w_slots = jnp.concatenate([cut(w_three, own, r, parts, 0) for r in order], axis=0)
    codes_k, codes_q = seg_codes(segment_ids)
    ranges = key_ranges(segment_ids, seq_count, K_CHUNK)
    ranges_back = key_ranges(segment_ids, seq_count, K_CHUNK_BACK)
    context, log_totals = attend(queries, keys, values, codes_q, codes_k, ranges, seq_count)

    out_slots = {slot: piece + context[0, 0] * 0 if slot else piece for slot, piece in out_slots.items()}
    out_slots = gather_slots(out_slots, "mp", [1])
    full_out = jnp.concatenate([out_slots[r] for r in range(parts)], axis=0)

    context_slots = exchange(context, own, "mp", 1)
    context_own = jnp.concatenate([context_slots[r] for r in range(parts)], axis=0)
    inputs_own = lax.dynamic_slice_in_dim(inputs, own * own_len, own_len, 1)
    first_sum = inputs_own.astype(F32) + (lead_dot(full_out, context_own) + bias_out[:, None])
    first_out, normed_first, inverse_one = norm_rows(first_sum, gain_first, shift_first)

    bias_up = b_up.astype(F32)[:, None]
    kept = []

    def forth(at, piece):
        kept[:], part = feed(at, length, list(kept), piece, up_turned, bias_up, down_turned)
        return part

    fed = gather_apply(first_out.astype(BF16), "mp", forth)
    all_first, all_active, all_slope = kept
    second_sum = first_out + (fed + bias_down[:, None])
    final_rows, normed_second, inverse_two = norm_rows(second_sum, gain_second, shift_second)

    grad_rows = cot_own.astype(F32)
    grad_shift_two = jnp.sum(grad_rows, axis=1)
    grad_gain_two = jnp.sum(grad_rows * normed_second, axis=1)
    second_grad = norm_back(grad_rows, normed_second, inverse_two, gain_second)
    grad_b_down = jnp.sum(second_grad, axis=1)

    kept_back = []

    def back(at, piece):
        kept_back[:], part = feed_back(at, length, list(kept_back), piece, all_slope, w_down, w_up)
        return part

    fed_back = gather_apply(second_grad.astype(BF16), "mp", back)
    all_down, all_up = kept_back
    grad_w_down = tail_dot(all_active, all_down).astype(BF16)
    grad_w_up = tail_dot(all_first, all_up).astype(BF16)
    grad_b_up = jnp.sum(all_up.astype(F32), axis=1)
    sum_down, sum_up = lax.psum((grad_w_down, grad_w_up), "dp")

    first_grad = second_grad + fed_back
    grad_shift_one = jnp.sum(first_grad, axis=1)
    grad_gain_one = jnp.sum(first_grad * normed_first, axis=1)
    attn_grad = norm_back(first_grad, normed_first, inverse_one, gain_first)
    grad_b_out = jnp.sum(attn_grad, axis=1)
    out_low = attn_grad.astype(BF16)
    context_grad = dot(full_out, out_low).astype(BF16)
    grad_heads = place(
        {r: swap(context_grad[r * width : (r + 1) * width], "mp", r) if r else context_grad[:width] for r in range(parts)},
        own,
        1,
    )
    late = grad_heads[0, 0] * 0
    final_low = final_rows.astype(BF16) + late
    twice = jnp.concatenate([final_low.reshape(parts, width, own_len), out_low.reshape(parts, width, own_len)], axis=1)
    back_here = place(exchange(twice.reshape(2 * D, own_len), own, "mp", 0), own, 1)
    layer_out, attn_here = back_here[:width], back_here[width:]
    stack_of = lambda slots: jnp.concatenate([slots[r] for r in order], axis=0)
    out_part = tail_dot(stack_of(context_slots), out_low).astype(BF16)
    grad_w_out = scatter_stack(out_part, "mp").astype(BF16)
    mixed = jnp.stack([grad_b_out, grad_gain_one, grad_shift_one, grad_b_down, grad_gain_two, grad_shift_two])
    mixed = scatter_stack(stack_of({r: cut(mixed, own, r, parts, 1) for r in range(parts)}), "mp", wire=F32)

    ready = (grad_w_down[0, 0] + grad_w_up[0, 0]) * 0
    all_grad = attend_back(
        queries, context, grad_heads + ready, log_totals, keys, values, codes_q, codes_k, ranges_back, seq_count
    )
    grad_biases = jnp.sum(all_grad.astype(F32), axis=0)
    grad_three = dot(inputs, all_grad)
    mixed = mixed + (back_here[0, 0] * 0).astype(F32)
    small = jnp.concatenate([mixed.reshape(-1), grad_biases[2 * width :], grad_biases[:width], grad_b_up])
    columns = 4 * width
    rows_small = 128
    small = jnp.concatenate([small, jnp.zeros((rows_small * columns - small.shape[0],), F32)]).reshape(rows_small, columns)
    packed = jnp.concatenate(
        [
            jnp.concatenate([grad_three.astype(BF16), grad_w_out.reshape(D, width)], axis=1),
            small.astype(BF16),
        ],
        axis=0,
    )
    input_part = tail_dot(w_slots + packed[0, 0] * 0, all_grad).astype(BF16)
    pieces, begun = sum_weights(packed, "dp")
    input_grad = (scatter_stack(input_part, "mp", late=begun) + attn_here.astype(F32)).astype(BF16)
    packed = jnp.concatenate(pieces, axis=0).astype(F32)
    small = packed[D:].reshape(-1)
    vec = [small[i * width : (i + 1) * width] for i in range(8)]
    sum_value, sum_key, sum_query = [packed[:D, i * width : (i + 1) * width] for i in range(3)]
    sum_out = packed[:D, 3 * width :].reshape(width, D)
    return (
        layer_out,
        input_grad,
        sum_query,
        vec[6],
        sum_key,
        sum_value,
        vec[7],
        sum_out,
        vec[0],
        vec[1],
        vec[2],
        sum_up.astype(F32),
        small[8 * width : 12 * width],
        sum_down.astype(F32),
        vec[3],
        vec[4],
        vec[5],
    )


def solution(mesh):
    in_specs = (
        P("mp", "dp"),
        P("dp"),
        P(None, "mp"),
        P("mp"),
        P(None, "mp"),
        P(None, "mp"),
        P("mp"),
        P("mp", None),
        P("mp"),
        P("mp"),
        P("mp"),
        P(None, "mp"),
        P("mp"),
        P("mp", None),
        P("mp"),
        P("mp"),
        P("mp"),
        P("mp", "dp"),
    )
    out_specs = (
        P("mp", "dp"),
        P("mp", "dp"),
        P(None, "mp"),
        P("mp"),
        P(None, "mp"),
        P(None, "mp"),
        P("mp"),
        P("mp", None),
        P("mp"),
        P("mp"),
        P("mp"),
        P(None, "mp"),
        P("mp"),
        P("mp", None),
        P("mp"),
        P("mp"),
        P("mp"),
    )
    return jax.shard_map(body, mesh=mesh, in_specs=in_specs, out_specs=out_specs, check_vma=False)
```

time: 653 us -> 561 us (0.86)
  waiting for transfers between devices: 268 us -> 154 us
  matrix products: 104 us -> 38.7 us
  Pallas kernels: 109 us -> 142 us
  between operations: 2.87 us -> 27.1 us
  local copies, waits for them, and re-layouts: 49.7 us -> 73.3 us
  other arithmetic: 38 us -> 59.7 us
  starting transfers between devices: 69.3 us -> 56 us
    ppermute x93 -> x59, waiting for transfers between devices: 268 us -> 148 us  [swap(): return lax.ppermute(piece, axis, [(i, i ^ mask) for i in range(count)])]
    pallas_call x0 -> x8, Pallas kernels: none -> 60 us  [the longest x4 31.2 us: feed(): pl.pallas_call(feed_kernel, grid=(blocks,), in_specs=[pl.BlockSpec((D, TO...]
    dot_general x12 -> x1, matrix products: 48.3 us -> 2.84 us  [lead_dot(): lax.dot_general(left, right, (((0,), (0,)), ((), ())), preferred_element_...]
    pallas_call x1, Pallas kernels: 57.7 us -> 32.1 us  [attend(): pl.pallas_call(lambda *refs: attend_kernel(heads, *refs), grid_spec=spec,...]
    slice x7 -> x31, local copies, waits for them, and re-layouts: 4.33 us -> 27 us  [the longest x4 4.94 us: scatter_stack(): sent = stack[half:].astype(wire)]
    add x5 -> x18, other arithmetic: 0.03 us -> 17.5 us  [the longest x3 5.05 us: scatter_stack(): stack = stack[:half].astype(F32) + moved.astype(F32)]
    dot_general x14 -> x3, matrix products: 31.3 us -> 15.6 us  [dot(): return jnp.dot(left, right, preferred_element_type=F32)]
    ppermute x93 -> x59, starting transfers between devices: 69.3 us -> 56 us  [swap(): return lax.ppermute(piece, axis, [(i, i ^ mask) for i in range(count)])]
  transfers between devices with their start and end apart: 93 -> 60, of which waited for: 47 -> 27; matrix products, arithmetic and copies ran while one was open for 22% -> 26% of each run, Pallas kernels for 17% -> 23%
where the time goes in v2:
time: 561 us; the launch traced here: 551 us
  waiting for transfers between devices  154 us (27%)
  Pallas kernels  142 us (25%)
  local copies, waits for them, and re-layouts  73.3 us (13%)
  other arithmetic  59.7 us (11%)
  starting transfers between devices  56 us (10%)
  matrix products  38.7 us (7%)
  between operations  27.1 us (5%)
    ppermute x59, waiting for transfers between devices, swap(): return lax.ppermute(piece, axis, [(i, i ^ mask) for i in range(count)])  148 us
    ppermute x59, starting transfers between devices, swap(): return lax.ppermute(piece, axis, [(i, i ^ mask) for i in range(count)])  56 us
    pallas_call x1, Pallas kernels, attend_back(): pl.pallas_call(lambda *refs: attend_back_kernel(heads, *refs), grid_spec=...  50.2 us
    pallas_call x1, Pallas kernels, attend(): pl.pallas_call(lambda *refs: attend_kernel(heads, *refs), grid_spec=spec,...  32.1 us
    pallas_call x4, Pallas kernels, feed(): pl.pallas_call(feed_kernel, grid=(blocks,), in_specs=[pl.BlockSpec((D, TO...  31.2 us
    pallas_call x4, Pallas kernels, feed_back(): pl.pallas_call(feed_back_kernel, grid=(blocks,), in_specs=[pl.BlockSpec((...  28.8 us
    dot_general x4, matrix products, tail_dot(): lax.dot_general(left, right, (((1,), (1,)), ((), ())), preferred_element_...  20.2 us
    unnamed x129, local copies, waits for them, and re-layouts  15.8 us
  transfers between devices with their start and end apart: 60, of which 27 were waited for; matrix products, arithmetic and copies ran while one was open for 26% of the time, Pallas kernels for 23%

profile of v2, /device:TPU:0, one launch (start us, length us, event | category | flops | bytes accessed | tf_op | source)
XLA Modules:
  0.0 550.8 jit_solution(6709533974165097528)
XLA Ops:
  24.4 10.0 %collective-permute-done.1 = bf16[256,2048]{1,0:T(8,128)(2,1)} collective-permute-done((bf16[256,2048]{1,0:T(8,128)(2,1)}, bf16[256,2048]{1,0:T(8,128)(2,1)}, u32[]{:S(2)}, u32[]{:S(2)}) %collective-permute-start.1) | collective-permute-done | bytes 1048608 | tf_op jit(solution)/shard_map/ppermute | solution.py:40
  44.5 5.9 %add_convert_fusion = bf16[768,2048]{1,0:T(8,128)(2,1)S(1)} fusion(bf16[1024,768]{1,0:T(8,128)(2,1)S(1)} %constant_dynamic-update-slice_fusion.29, bf16[1024,2048]{1,0:T(8,128)(2,1)} %constant_dynamic-update-slice_fusion.25, f32[768]{0:T(1024)S(1)} %maximum_convert_fusion.2), kind=kOutput, calls=%fused_computation | convolution fusion | flops 3224371200 | bytes 8915968 | tf_op jit(solution)/shard_map/dot_general | solution.py:35
  52.2 32.1 %attend.1 = (bf16[256,2048]{1,0:T(8,128)(2,1)}, f32[1,4,2048]{2,1,0:T(4,128)}) custom-call(s32[4]{0:T(128)} %get-tuple-element.186.refs_0_, s32[4]{0:T(128)} %get-tuple-element.181.refs_1_, bf16[256,2048]{1,0:T(8,128)(2,1)} %get-tuple-element.117.refs_2_, bf16[256,2048]{1,0:T(8,128)(2,1)} %get-tuple-element.116.refs_3_.refs_6_, ...), custom_call_target="tpu_custom_call" | custom-call | flops 12884901888 | bytes 4194304 | tf_op jit(solution)/shard_map/attend/pallas_call | solution.py:295
  90.6 6.8 %collective-permute-done.7 = bf16[256,512]{1,0:T(8,128)(2,1)S(1)} collective-permute-done((bf16[256,512]{1,0:T(8,128)(2,1)S(1)}, bf16[256,512]{1,0:T(8,128)(2,1)S(1)}, u32[]{:S(2)}, u32[]{:S(2)}) %collective-permute-start.7) | collective-permute-done | bytes 262176 | tf_op jit(solution)/shard_map/ppermute | solution.py:40
  97.4 4.5 collective-permute-done.8
  110.1 4.0 copy.68
  115.1 7.7 %feed.4 = (bf16[1024,2048]{1,0:T(8,128)(2,1)}, bf16[1024,2048]{1,0:T(8,128)(2,1)}, bf16[1024,2048]{1,0:T(8,128)(2,1)}, bf16[1024,512]{1,0:T(8,128)(2,1)}) custom-call(bf16[1024,512]{1,0:T(8,128)(2,1)} %fusion.10.y_ref, bf16[1024,1024]{1,0:T(8,128)(2,1)} %bitcast.50, f32[1024,1]{1,0:T(8,128)} %copy.69.bias_ref, bf16[1024,1024]{1,0:T(8,128)(2,1)} %bitcast.54), custom_call_target="tpu_custom_call" | custom-call | flops 2147483648 | bytes 8388608 | tf_op jit(solution)/shard_map/feed/pallas_call | solution.py:446
  122.8 7.8 %feed.5 = (bf16[1024,2048]{1,0:T(8,128)(2,1)}, bf16[1024,2048]{1,0:T(8,128)(2,1)}, bf16[1024,2048]{1,0:T(8,128)(2,1)}, bf16[1024,512]{1,0:T(8,128)(2,1)}) custom-call(bf16[1024,512]{1,0:T(8,128)(2,1)} %collective-permute-done.12.y_ref, bf16[1024,1024]{1,0:T(8,128)(2,1)} %bitcast.51, ...), custom_call_target="tpu_custom_call", output_to_operand_aliasing={{0}: (4, {}), {1}: (5, {}), {2}: (6, {})} | custom-call | flops 2147483648 | bytes 8388608 | tf_op jit(solution)/shard_map/feed/pallas_call | solution.py:446
  136.4 8.0 %feed.6 = (bf16[1024,2048]{1,0:T(8,128)(2,1)}, bf16[1024,2048]{1,0:T(8,128)(2,1)}, bf16[1024,2048]{1,0:T(8,128)(2,1)}, bf16[1024,512]{1,0:T(8,128)(2,1)}) custom-call(bf16[1024,512]{1,0:T(8,128)(2,1)} %pad_maximum_fusion.8.y_ref, bf16[1024,1024]{1,0:T(8,128)(2,1)} %bitcast.52, ...), custom_call_target="tpu_custom_call", output_to_operand_aliasing={{0}: (4, {}), {1}: (5, {}), {2}: (6, {})} | custom-call | flops 2147483648 | bytes 8388608 | tf_op jit(solution)/shard_map/feed/pallas_call | solution.py:446
  151.0 7.7 %feed.7 = (bf16[1024,2048]{1,0:T(8,128)(2,1)}, bf16[1024,2048]{1,0:T(8,128)(2,1)}, bf16[1024,2048]{1,0:T(8,128)(2,1)}, bf16[1024,512]{1,0:T(8,128)(2,1)}) custom-call(bf16[1024,512]{1,0:T(8,128)(2,1)} %pad_maximum_fusion.9.y_ref, bf16[1024,1024]{1,0:T(8,128)(2,1)} %bitcast.53, ...), custom_call_target="tpu_custom_call", output_to_operand_aliasing={{0}: (4, {}), {1}: (5, {}), {2}: (6, {})} | custom-call | flops 2147483648 | bytes 8388608 | tf_op jit(solution)/shard_map/feed/pallas_call | solution.py:446
  158.8 4.0 collective-permute-done.17
  172.6 18.0 %collective-permute-done.21 = bf16[256,512]{1,0:T(8,128)(2,1)S(1)} collective-permute-done((bf16[256,512]{1,0:T(8,128)(2,1)S(1)}, bf16[256,512]{1,0:T(8,128)(2,1)S(1)}, u32[]{:S(2)}, u32[]{:S(2)}) %collective-permute-start.21) | collective-permute-done | bytes 262176 | tf_op jit(solution)/shard_map/ppermute | solution.py:40
  190.6 4.0 collective-permute-done.22
  200.5 7.0 %feed_back.4 = (bf16[1024,2048]{1,0:T(8,128)(2,1)}, bf16[1024,2048]{1,0:T(8,128)(2,1)}, bf16[1024,512]{1,0:T(8,128)(2,1)}) custom-call(bf16[1024,512]{1,0:T(8,128)(2,1)} %copy-done.10, bf16[1024,2048]{1,0:T(8,128)(2,1)} %get-tuple-element.61.slope_ref, bf16[1024,1024]{1,0:T(8,128)(2,1)} %down_ref.7, bf16[1024,1024]{1,0:T(8,128)(2,1)} %up_ref.7), custom_call_target="tpu_custom_call" | custom-call | flops 2147483648 | bytes 8388608 | tf_op jit(solution)/shard_map/feed_back/pallas_call | solution.py:502
  208.5 7.1 %feed_back.5 = (bf16[1024,2048]{1,0:T(8,128)(2,1)}, bf16[1024,2048]{1,0:T(8,128)(2,1)}, bf16[1024,512]{1,0:T(8,128)(2,1)}) custom-call(bf16[1024,512]{1,0:T(8,128)(2,1)} %copy-done.19, bf16[1024,2048]{1,0:T(8,128)(2,1)} %get-tuple-element.61.slope_ref, bf16[1024,1024]{1,0:T(8,128)(2,1)} %down_ref.7, ...), custom_call_target="tpu_custom_call", output_to_operand_aliasing={{0}: (4, {}), {1}: (5, {})} | custom-call | flops 2147483648 | bytes 8388608 | tf_op jit(solution)/shard_map/feed_back/pallas_call | solution.py:502
  217.4 7.1 %collective-permute-done.25 = bf16[1024,512]{1,0:T(8,128)(2,1)S(1)} collective-permute-done((bf16[1024,512]{1,0:T(8,128)(2,1)S(1)}, bf16[1024,512]{1,0:T(8,128)(2,1)S(1)}, u32[]{:S(2)}, u32[]{:S(2)}) %collective-permute-start.25) | collective-permute-done | bytes 1048608 | tf_op jit(solution)/shard_map/ppermute | solution.py:40
  229.2 7.5 %feed_back.6 = (bf16[1024,2048]{1,0:T(8,128)(2,1)}, bf16[1024,2048]{1,0:T(8,128)(2,1)}, bf16[1024,512]{1,0:T(8,128)(2,1)}) custom-call(bf16[1024,512]{1,0:T(8,128)(2,1)} %pad_maximum_fusion.10.m_ref, bf16[1024,2048]{1,0:T(8,128)(2,1)} %get-tuple-element.61.slope_ref, bf16[1024,1024]{1,0:T(8,128)(2,1)} %down_ref.7, ...), custom_call_target="tpu_custom_call", output_to_operand_aliasing={{0}: (4, {}), {1}: (5, {})} | custom-call | flops 2147483648 | bytes 8388608 | tf_op jit(solution)/shard_map/feed_back/pallas_call | solution.py:502
  246.4 7.2 %feed_back.7 = (bf16[1024,2048]{1,0:T(8,128)(2,1)}, bf16[1024,2048]{1,0:T(8,128)(2,1)}, bf16[1024,512]{1,0:T(8,128)(2,1)}) custom-call(bf16[1024,512]{1,0:T(8,128)(2,1)} %pad_maximum_fusion.11.m_ref, bf16[1024,2048]{1,0:T(8,128)(2,1)} %get-tuple-element.61.slope_ref, bf16[1024,1024]{1,0:T(8,128)(2,1)} %down_ref.7, ...), custom_call_target="tpu_custom_call", output_to_operand_aliasing={{0}: (4, {}), {1}: (5, {})} | custom-call | flops 2147483648 | bytes 8388608 | tf_op jit(solution)/shard_map/feed_back/pallas_call | solution.py:502
  259.0 8.1 %convolution_convert_fusion.2 = bf16[1024,1024]{1,0:T(8,128)(2,1)} fusion(bf16[1024,2048]{1,0:T(8,128)(2,1)S(1)} %copy-done.5, bf16[1024,2048]{1,0:T(8,128)(2,1)} %get-tuple-element.75), kind=kOutput, calls=%fused_computation.37 | convolution fusion | flops 4296015872 | bytes 10485760 | tf_op jit(solution)/shard_map/dot_general | solution.py:31
  269.2 5.7 %convolution_convert_fusion.3 = bf16[1024,1024]{1,0:T(8,128)(2,1)} fusion(bf16[1024,2048]{1,0:T(8,128)(2,1)S(1)} %copy-done.6, bf16[1024,2048]{1,0:T(8,128)(2,1)S(1)} %copy-done.4), kind=kOutput, calls=%fused_computation.38 | convolution fusion | flops 4296015872 | bytes 10485760 | tf_op jit(solution)/shard_map/dot_general | solution.py:31
  315.7 50.2 %attend_back.1 = bf16[2048,768]{1,0:T(8,128)(2,1)} custom-call(s32[4]{0:T(128)} %get-tuple-element.187.refs_0_, s32[4]{0:T(128)} %get-tuple-element.180.refs_1_, bf16[256,2048]{1,0:T(8,128)(2,1)} %get-tuple-element.117.refs_2_, bf16[256,2048]{1,0:T(8,128)(2,1)} %get-tuple-element.47.refs_3_, bf16[256,2048]{1,0:T(8,128)(2,1)} %broadcast_add_fusion.refs_4_, ...), custom_call_target="tpu_custom_call" | custom-call | flops 32212254720 | bytes 7340032 | tf_op jit(solution)/shard_map/attend_back/pallas_call | solution.py:405
  365.9 7.0 %convolution_convert_fusion.4 = bf16[1024,768]{1,0:T(8,128)(2,1)S(1)} fusion(bf16[1024,2048]{1,0:T(8,128)(2,1)} %constant_dynamic-update-slice_fusion.25, bf16[2048,768]{1,0:T(8,128)(2,1)} %attend_back.1), kind=kOutput, calls=%fused_computation.41 | convolution fusion | flops 3222011904 | bytes 8912896 | tf_op jit(solution)/shard_map/dot_general | solution.py:35
  375.2 5.1 convolution_convert_fusion
  396.7 11.8 %collective-permute-done.39 = bf16[256,1024]{1,0:T(8,128)(2,1)} collective-permute-done((bf16[256,1024]{1,0:T(8,128)(2,1)S(1)}, bf16[256,1024]{1,0:T(8,128)(2,1)}, u32[]{:S(2)}, u32[]{:S(2)}) %collective-permute-start.39) | collective-permute-done | bytes 524320 | tf_op jit(solution)/shard_map/ppermute | solution.py:40
  421.5 14.3 %collective-permute-done.43 = bf16[96,1024]{1,0:T(8,128)(2,1)} collective-permute-done((bf16[96,1024]{1,0:T(8,128)(2,1)}, bf16[96,1024]{1,0:T(8,128)(2,1)}, u32[]{:S(2)}, u32[]{:S(2)}) %collective-permute-start.43) | collective-permute-done | bytes 196640 | tf_op jit(solution)/shard_map/ppermute | solution.py:40
  435.8 3.9 collective-permute-done.44
  439.7 6.5 %collective-permute-done.45 = bf16[96,1024]{1,0:T(8,128)(2,1)} collective-permute-done((bf16[96,1024]{1,0:T(8,128)(2,1)}, bf16[96,1024]{1,0:T(8,128)(2,1)}, u32[]{:S(2)}, u32[]{:S(2)}) %collective-permute-start.45) | collective-permute-done | bytes 196640 | tf_op jit(solution)/shard_map/ppermute | solution.py:40
  449.3 5.5 all-reduce.3.cloned.1.call-done
  454.8 4.2 convert_element_type.364
  479.9 10.0 %collective-permute-done.48 = bf16[96,1024]{1,0:T(8,128)(2,1)S(1)} collective-permute-done((bf16[96,1024]{1,0:T(8,128)(2,1)S(1)}, bf16[96,1024]{1,0:T(8,128)(2,1)S(1)}, u32[]{:S(2)}, u32[]{:S(2)}) %collective-permute-start.48) | collective-permute-done | bytes 196640 | tf_op jit(solution)/shard_map/ppermute | solution.py:40
  500.8 11.3 %collective-permute-done.52 = bf16[96,1024]{1,0:T(8,128)(2,1)S(1)} collective-permute-done((bf16[96,1024]{1,0:T(8,128)(2,1)S(1)}, bf16[96,1024]{1,0:T(8,128)(2,1)S(1)}, u32[]{:S(2)}, u32[]{:S(2)}) %collective-permute-start.52) | collective-permute-done | bytes 196640 | tf_op jit(solution)/shard_map/ppermute | solution.py:40
  524.6 8.7 %collective-permute-done.57 = bf16[96,1024]{1,0:T(8,128)(2,1)S(1)} collective-permute-done((bf16[96,1024]{1,0:T(8,128)(2,1)S(1)}, bf16[96,1024]{1,0:T(8,128)(2,1)S(1)}, u32[]{:S(2)}, u32[]{:S(2)}) %collective-permute-start.57) | collective-permute-done | bytes 196640 | tf_op jit(solution)/shard_map/ppermute | solution.py:40
  (398 shorter events, 215.1 us)
Async XLA Ops:
  7.2 31.7 %collective-permute-start = (bf16[256,2048]{1,0:T(8,128)(2,1)}, bf16[256,2048]{1,0:T(8,128)(2,1)}, u32[]{:S(2)}, u32[]{:S(2)}) collective-permute-start(bf16[256,2048]{1,0:T(8,128)(2,1)} %param.18), channel_id=1, source_target_pairs={{0,1},{1,0},{2,3},{3,2},{4,5},{5,4},{6,7},{7,6},{8,9},{9,8},{10,11... | collective-permute-start | bytes 3145736 | tf_op jit(solution)/shard_map/ppermute | solution.py:40
  7.7 26.7 %collective-permute-start.1 = (bf16[256,2048]{1,0:T(8,128)(2,1)}, bf16[256,2048]{1,0:T(8,128)(2,1)}, u32[]{:S(2)}, u32[]{:S(2)}) collective-permute-start(bf16[256,2048]{1,0:T(8,128)(2,1)} %param.18), channel_id=1, source_target_pairs={{0,2},{1,3},{2,0},{3,1},{4,6},{5,7},{6,4},{7,5},{8,10},{9,11},{10,... | collective-permute-start | bytes 3145736 | tf_op jit(solution)/shard_map/ppermute | solution.py:40
  14.3 20.8 %collective-permute-start.9 = (bf16[6,256]{1,0:T(8,128)(2,1)S(1)}, bf16[6,256]{1,0:T(8,128)(2,1)S(1)}, u32[]{:S(2)}, u32[]{:S(2)}) collective-permute-start(bf16[6,256]{1,0:T(8,128)(2,1)S(1)} %stack.48), channel_id=1, source_target_pairs={{0,1},{1,0},{2,3},{3,2},{4,5},{5,4},{6,7},{7,6},{8,9},{9,8},{10,11... | collective-permute-start | bytes 9224 | tf_op jit(solution)/shard_map/ppermute | solution.py:40
  14.5 20.0 %collective-permute-start.10 = (bf16[6,256]{1,0:T(8,128)(2,1)S(1)}, bf16[6,256]{1,0:T(8,128)(2,1)S(1)}, u32[]{:S(2)}, u32[]{:S(2)}) collective-permute-start(bf16[6,256]{1,0:T(8,128)(2,1)S(1)} %stack.48), channel_id=1, source_target_pairs={{0,2},{1,3},{2,0},{3,1},{4,6},{5,7},{6,4},{7,5},{8,10},{9,11},{10,... | collective-permute-start | bytes 9224 | tf_op jit(solution)/shard_map/ppermute | solution.py:40
  34.5 54.0 %collective-permute-start.11 = (bf16[6,256]{1,0:T(8,128)(2,1)S(1)}, bf16[6,256]{1,0:T(8,128)(2,1)S(1)}, u32[]{:S(2)}, u32[]{:S(2)}) collective-permute-start(bf16[6,256]{1,0:T(8,128)(2,1)S(1)} %collective-permute-done.10), channel_id=1, source_target_pairs={{0,1},{1,0},{2,3},{3,2},{4,5},{5,4},{6,7},{7,6},{8,9},{9,8},{10,11... | collective-permute-start | bytes 9224 | tf_op jit(solution)/shard_map/ppermute | solution.py:40
  37.0 49.1 %collective-permute-start.4 = (bf16[256,1024]{1,0:T(8,128)(2,1)S(1)}, bf16[256,1024]{1,0:T(8,128)(2,1)S(1)}, u32[]{:S(2)}, u32[]{:S(2)}) collective-permute-start(bf16[256,1024]{1,0:T(8,128)(2,1)S(1)} %broadcast_add_fusion.5), channel_id=1, source_target_pairs={{0,2},{1,3},{2,0},{3,1},{4,6},{5,7},{6,4},{7,5},{8,10},{9,11},{10,... | collective-permute-start | bytes 1572872 | tf_op jit(solution)/shard_map/ppermute | solution.py:40
  38.9 51.7 %collective-permute-start.3 = (bf16[256,1024]{1,0:T(8,128)(2,1)S(1)}, bf16[256,1024]{1,0:T(8,128)(2,1)S(1)}, u32[]{:S(2)}, u32[]{:S(2)}) collective-permute-start(bf16[256,1024]{1,0:T(8,128)(2,1)S(1)} %broadcast_add_fusion.5), channel_id=1, source_target_pairs={{0,1},{1,0},{2,3},{3,2},{4,5},{5,4},{6,7},{7,6},{8,9},{9,8},{10,11... | collective-permute-start | bytes 1572872 | tf_op jit(solution)/shard_map/ppermute | solution.py:40
  86.2 15.7 %collective-permute-start.5 = (bf16[256,1024]{1,0:T(8,128)(2,1)S(1)}, bf16[256,1024]{1,0:T(8,128)(2,1)S(1)}, u32[]{:S(2)}, u32[]{:S(2)}) collective-permute-start(bf16[256,1024]{1,0:T(8,128)(2,1)S(1)} %broadcast_add_fusion.4), channel_id=1, source_target_pairs={{0,1},{1,0},{2,3},{3,2},{4,5},{5,4},{6,7},{7,6},{8,9},{9,8},{10,11... | collective-permute-start | bytes 1572872 | tf_op jit(solution)/shard_map/ppermute | solution.py:40
  106.5 16.3 %collective-permute-start.12 = (bf16[1024,512]{1,0:T(8,128)(2,1)}, bf16[1024,512]{1,0:T(8,128)(2,1)}, u32[]{:S(2)}, u32[]{:S(2)}) collective-permute-start(bf16[1024,512]{1,0:T(8,128)(2,1)} %fusion.10.y_ref), channel_id=1, source_target_pairs={{0,1},{1,0},{2,3},{3,2},{4,5},{5,4},{6,7},{7,6},{8,9},{9,8},{10,11... | collective-permute-start | bytes 3145736 | tf_op jit(solution)/shard_map/ppermute | solution.py:40
  106.9 25.5 %collective-permute-start.14 = (bf16[1024,512]{1,0:T(8,128)(2,1)}, bf16[1024,512]{1,0:T(8,128)(2,1)S(1)}, u32[]{:S(2)}, u32[]{:S(2)}) collective-permute-start(bf16[1024,512]{1,0:T(8,128)(2,1)} %fusion.10.y_ref), channel_id=1, source_target_pairs={{0,2},{1,3},{2,0},{3,1},{4,6},{5,7},{6,4},{7,5},{8,10},{9,11},{10,... | collective-permute-start | bytes 3145736 | tf_op jit(solution)/shard_map/ppermute | solution.py:40
  166.0 28.6 %collective-permute-start.13 = (bf16[1024,512]{1,0:T(8,128)(2,1)}, bf16[1024,512]{1,0:T(8,128)(2,1)S(1)}, u32[]{:S(2)}, u32[]{:S(2)}) collective-permute-start(bf16[1024,512]{1,0:T(8,128)(2,1)} %get-tuple-element.52), channel_id=1, source_target_pairs={{0,1},{1,0},{2,3},{3,2},{4,5},{5,4},{6,7},{7,6},{8,9},{9,8},{10,11... | collective-permute-start | bytes 3145736 | tf_op jit(solution)/shard_map/ppermute | solution.py:40
  170.2 24.5 %collective-permute-start.19 = (bf16[1024,256]{1,0:T(8,128)(2,1)S(1)}, bf16[1024,256]{1,0:T(8,128)(2,1)S(1)}, u32[]{:S(2)}, u32[]{:S(2)}) collective-permute-start(bf16[1024,256]{1,0:T(8,128)(2,1)S(1)} %add_convert_fusion.4), channel_id=1, source_target_pairs={{0,2},{1,3},{2,0},{3,1},{4,6},{5,7},{6,4},{7,5},{8,10},{9,11},{10,... | collective-permute-start | bytes 1572872 | tf_op jit(solution)/shard_map/ppermute | solution.py:40
  171.4 19.2 %collective-permute-start.21 = (bf16[256,512]{1,0:T(8,128)(2,1)S(1)}, bf16[256,512]{1,0:T(8,128)(2,1)S(1)}, u32[]{:S(2)}, u32[]{:S(2)}) collective-permute-start(bf16[256,512]{1,0:T(8,128)(2,1)S(1)} %get-tuple-element.147), channel_id=1, source_target_pairs={{0,2},{1,3},{2,0},{3,1},{4,6},{5,7},{6,4},{7,5},{8,10},{9,11},{10,... | collective-permute-start | bytes 786440 | tf_op jit(solution)/shard_map/ppermute | solution.py:40
  172.2 22.4 %collective-permute-start.22 = (bf16[256,512]{1,0:T(8,128)(2,1)S(1)}, bf16[256,512]{1,0:T(8,128)(2,1)S(1)}, u32[]{:S(2)}, u32[]{:S(2)}) collective-permute-start(bf16[256,512]{1,0:T(8,128)(2,1)S(1)} %get-tuple-element.144), channel_id=1, source_target_pairs={{0,3},{1,2},{2,1},{3,0},{4,7},{5,6},{6,5},{7,4},{8,11},{9,10},{10,... | collective-permute-start | bytes 786440 | tf_op jit(solution)/shard_map/ppermute | solution.py:40
  199.3 25.1 %collective-permute-start.25 = (bf16[1024,512]{1,0:T(8,128)(2,1)S(1)}, bf16[1024,512]{1,0:T(8,128)(2,1)S(1)}, u32[]{:S(2)}, u32[]{:S(2)}) collective-permute-start(bf16[1024,512]{1,0:T(8,128)(2,1)S(1)} %fusion.40.m_ref), channel_id=1, source_target_pairs={{0,2},{1,3},{2,0},{3,1},{4,6},{5,7},{6,4},{7,5},{8,10},{9,11},{10,... | collective-permute-start | bytes 3145736 | tf_op jit(solution)/shard_map/ppermute | solution.py:40
  245.3 36.6 %collective-permute-start.24 = (bf16[1024,512]{1,0:T(8,128)(2,1)}, bf16[1024,512]{1,0:T(8,128)(2,1)}, u32[]{:S(2)}, u32[]{:S(2)}) collective-permute-start(bf16[1024,512]{1,0:T(8,128)(2,1)} %get-tuple-element.65), channel_id=1, source_target_pairs={{0,1},{1,0},{2,3},{3,2},{4,5},{5,4},{6,7},{7,6},{8,9},{9,8},{10,11... | collective-permute-start | bytes 3145736 | tf_op jit(solution)/shard_map/ppermute | solution.py:40
  277.3 177.6 %all-reduce.3.cloned.1.call-start = ((), (), s32[]{:S(2)}) async-start(), calls=%async_computation | async-start | bytes 8388608 | tf_op jit(solution)/shard_map/psum | solution.py:637
  299.6 91.4 %collective-permute-start.38 = (bf16[512,1024]{1,0:T(8,128)(2,1)}, bf16[512,1024]{1,0:T(8,128)(2,1)}, u32[]{:S(2)}, u32[]{:S(2)}) collective-permute-start(bf16[512,1024]{1,0:T(8,128)(2,1)} %slice.399), channel_id=1, source_target_pairs={{0,1},{1,0},{2,3},{3,2},{4,5},{5,4},{6,7},{7,6},{8,9},{9,8},{10,11... | collective-permute-start | bytes 3145736 | tf_op jit(solution)/shard_map/ppermute | solution.py:40
  301.0 88.3 %collective-permute-start.42 = (f32[6,256]{1,0:T(8,128)}, f32[6,256]{1,0:T(8,128)}, u32[]{:S(2)}, u32[]{:S(2)}) collective-permute-start(f32[6,256]{1,0:T(8,128)} %slice.404), channel_id=1, source_target_pairs={{0,2},{1,3},{2,0},{3,1},{4,6},{5,7},{6,4},{7,5},{8,10},{9,11},{10,... | collective-permute-start | bytes 18440 | tf_op jit(solution)/shard_map/ppermute | solution.py:40
  312.1 73.9 %collective-permute-start.34 = (bf16[512,512]{1,0:T(8,128)(2,1)}, bf16[512,512]{1,0:T(8,128)(2,1)}, u32[]{:S(2)}, u32[]{:S(2)}) collective-permute-start(bf16[512,512]{1,0:T(8,128)(2,1)} %get-tuple-element.122), channel_id=1, source_target_pairs={{0,1},{1,0},{2,3},{3,2},{4,5},{5,4},{6,7},{7,6},{8,9},{9,8},{10,11... | collective-permute-start | bytes 1572872 | tf_op jit(solution)/shard_map/ppermute | solution.py:40
  313.3 74.7 %collective-permute-start.35 = (bf16[512,512]{1,0:T(8,128)(2,1)}, bf16[512,512]{1,0:T(8,128)(2,1)S(1)}, u32[]{:S(2)}, u32[]{:S(2)}) collective-permute-start(bf16[512,512]{1,0:T(8,128)(2,1)} %get-tuple-element.121), channel_id=1, source_target_pairs={{0,2},{1,3},{2,0},{3,1},{4,6},{5,7},{6,4},{7,5},{8,10},{9,11},{10,... | collective-permute-start | bytes 1572872 | tf_op jit(solution)/shard_map/ppermute | solution.py:40
  314.4 73.6 %collective-permute-start.36 = (bf16[512,512]{1,0:T(8,128)(2,1)}, bf16[512,512]{1,0:T(8,128)(2,1)S(1)}, u32[]{:S(2)}, u32[]{:S(2)}) collective-permute-start(bf16[512,512]{1,0:T(8,128)(2,1)} %get-tuple-element.120), channel_id=1, source_target_pairs={{0,3},{1,2},{2,1},{3,0},{4,7},{5,6},{6,5},{7,4},{8,11},{9,10},{10,... | collective-permute-start | bytes 1572872 | tf_op jit(solution)/shard_map/ppermute | solution.py:40
  385.9 81.9 %collective-permute-start.37 = (bf16[512,2048]{1,0:T(8,128)(2,1)}, bf16[512,2048]{1,0:T(8,128)(2,1)}, u32[]{:S(2)}, u32[]{:S(2)}) collective-permute-start(bf16[512,2048]{1,0:T(8,128)(2,1)} %slice.395), channel_id=1, source_target_pairs={{0,1},{1,0},{2,3},{3,2},{4,5},{5,4},{6,7},{7,6},{8,9},{9,8},{10,11... | collective-permute-start | bytes 6291464 | tf_op jit(solution)/shard_map/ppermute | solution.py:40
  413.7 47.8 %collective-permute-start.40 = (bf16[384,1024]{1,0:T(8,128)(2,1)}, bf16[384,1024]{1,0:T(8,128)(2,1)}, u32[]{:S(2)}, u32[]{:S(2)}) collective-permute-start(bf16[384,1024]{1,0:T(8,128)(2,1)} %get-tuple-element.118), channel_id=1, source_target_pairs={{0,4},{4,0},{8,12},{12,8},{16,20},{20,16},{24,28},{28,24},{1,5},{5... | collective-permute-start | bytes 2359304 | tf_op jit(solution)/shard_map/ppermute | solution.py:40
  416.1 19.7 %collective-permute-start.43 = (bf16[96,1024]{1,0:T(8,128)(2,1)}, bf16[96,1024]{1,0:T(8,128)(2,1)}, u32[]{:S(2)}, u32[]{:S(2)}) collective-permute-start(bf16[96,1024]{1,0:T(8,128)(2,1)} %get-tuple-element.155), channel_id=1, source_target_pairs={{0,8},{4,12},{8,0},{12,4},{16,24},{20,28},{24,16},{28,20},{1,9},{5... | collective-permute-start | bytes 589832 | tf_op jit(solution)/shard_map/ppermute | solution.py:40
  416.1 23.6 %collective-permute-start.44 = (bf16[96,1024]{1,0:T(8,128)(2,1)}, bf16[96,1024]{1,0:T(8,128)(2,1)}, u32[]{:S(2)}, u32[]{:S(2)}) collective-permute-start(bf16[96,1024]{1,0:T(8,128)(2,1)} %get-tuple-element.156), channel_id=1, source_target_pairs={{0,16},{4,20},{8,24},{12,28},{16,0},{20,4},{24,8},{28,12},{1,17},{... | collective-permute-start | bytes 589832 | tf_op jit(solution)/shard_map/ppermute | solution.py:40
  418.3 27.9 %collective-permute-start.45 = (bf16[96,1024]{1,0:T(8,128)(2,1)}, bf16[96,1024]{1,0:T(8,128)(2,1)}, u32[]{:S(2)}, u32[]{:S(2)}) collective-permute-start(bf16[96,1024]{1,0:T(8,128)(2,1)} %get-tuple-element.157), channel_id=1, source_target_pairs={{0,24},{4,28},{8,16},{12,20},{16,8},{20,12},{24,0},{28,4},{1,25},{... | collective-permute-start | bytes 589832 | tf_op jit(solution)/shard_map/ppermute | solution.py:40
  473.9 15.9 %collective-permute-start.48 = (bf16[96,1024]{1,0:T(8,128)(2,1)S(1)}, bf16[96,1024]{1,0:T(8,128)(2,1)S(1)}, u32[]{:S(2)}, u32[]{:S(2)}) collective-permute-start(bf16[96,1024]{1,0:T(8,128)(2,1)S(1)} %get-tuple-element.154), channel_id=1, source_target_pairs={{0,16},{4,20},{8,24},{12,28},{16,0},{20,4},{24,8},{28,12},{1,17},{... | collective-permute-start | bytes 589832 | tf_op jit(solution)/shard_map/ppermute | solution.py:40
  474.2 15.7 %collective-permute-start.49 = (bf16[96,1024]{1,0:T(8,128)(2,1)S(1)}, bf16[96,1024]{1,0:T(8,128)(2,1)S(1)}, u32[]{:S(2)}, u32[]{:S(2)}) collective-permute-start(bf16[96,1024]{1,0:T(8,128)(2,1)S(1)} %get-tuple-element.153), channel_id=1, source_target_pairs={{0,24},{4,28},{8,16},{12,20},{16,8},{20,12},{24,0},{28,4},{1,25},{... | collective-permute-start | bytes 589832 | tf_op jit(solution)/shard_map/ppermute | solution.py:40
  495.9 37.5 %collective-permute-start.46 = (bf16[256,2048]{1,0:T(8,128)(2,1)S(1)}, bf16[256,2048]{1,0:T(8,128)(2,1)S(1)}, u32[]{:S(2)}, u32[]{:S(2)}) collective-permute-start(bf16[256,2048]{1,0:T(8,128)(2,1)S(1)} %fusion.21), channel_id=1, source_target_pairs={{0,2},{1,3},{2,0},{3,1},{4,6},{5,7},{6,4},{7,5},{8,10},{9,11},{10,... | collective-permute-start | bytes 3145736 | tf_op jit(solution)/shard_map/ppermute | solution.py:40
  516.2 17.2 %collective-permute-start.57 = (bf16[96,1024]{1,0:T(8,128)(2,1)S(1)}, bf16[96,1024]{1,0:T(8,128)(2,1)S(1)}, u32[]{:S(2)}, u32[]{:S(2)}) collective-permute-start(bf16[96,1024]{1,0:T(8,128)(2,1)S(1)} %get-tuple-element.96), channel_id=1, source_target_pairs={{0,16},{4,20},{8,24},{12,28},{16,0},{20,4},{24,8},{28,12},{1,17},{... | collective-permute-start | bytes 589832 | tf_op jit(solution)/shard_map/ppermute | solution.py:40
  519.6 19.0 %collective-permute-start.55 = (bf16[384,1024]{1,0:T(8,128)(2,1)S(1)}, bf16[384,1024]{1,0:T(8,128)(2,1)S(1)}, u32[]{:S(2)}, u32[]{:S(2)}) collective-permute-start(bf16[384,1024]{1,0:T(8,128)(2,1)S(1)} %get-tuple-element.94), channel_id=1, source_target_pairs={{0,4},{4,0},{8,12},{12,8},{16,20},{20,16},{24,28},{28,24},{1,5},{5... | collective-permute-start | bytes 2359304 | tf_op jit(solution)/shard_map/ppermute | solution.py:40
  (88 other events, 820.5 us)
Sparse Core Ops, SparseCore 0:
  281.8 172.9 all-reduce.2
